TPU v7x, 256 devices: a whole 4x4x8 slice. The times are simulated.
256 devices in a mesh: row: 16 (over y_lo, z), tp: 16 (over x, y_hi, core).
Axes of the slice: x: 4, y: 4 (y_hi: 2, y_lo: 2; y = y_hi * 2 + y_lo), z: 8, core: 2. Of those that a mesh axis runs over, the one named last changes fastest.
Arguments:
- feature_map: bfloat16 [1, 128, 128, 4096], P(None, 'row', None, 'tp'), may hold values from -6 to 6
- conv_weight: bfloat16 [3, 64, 64, 576], P(None, 'tp'), may hold values from -0.25 to 0.25
- branch_bias: float32 [3, 4096], P(None, 'tp'), may hold values from -3 to 3
- unite_weight: bfloat16 [3, 4096, 1024], P(None, 'tp'), may hold values from -0.0546875 to 0.0546875
Outputs:
- head_out: bfloat16 [1, 128, 128, 1024], P(None, 'row', 'tp')
All inputs are finite; a program needn't handle non-finite values.
Results may differ from a plain program's by a relative error of at most 0.0049.
Values may be sent and summed in bfloat16 or wider, within the bound.
No kernel may reach another device: no remote copies, remote signals or barrier semaphores. Data moves between devices by JAX's collectives and lax.ppermute only.
A program may use at most 64 MiB of HBM per device.

v0:
```python
import jax
import jax.numpy as jnp
from jax import lax
from jax.sharding import PartitionSpec as P


def from_behind(array, axis, by):
    length = lax.axis_size(axis)
    pairs = [(i, i + by) for i in range(length) if 0 <= i + by < length]
    return lax.ppermute(array, axis, pairs)


def column_view(source_map, offset):
    col_count = source_map.shape[2]
    border_width = abs(offset)
    padded = jnp.pad(source_map, ((0, 0), (0, 0), (border_width, border_width), (0, 0)))
    start_col = border_width + offset
    return lax.slice_in_dim(padded, start_col, start_col + col_count, axis=2)


def block_kernels(kernel):
    group_count, group_width, tap_width = kernel.shape
    split = kernel.astype(jnp.float32).reshape(group_count, group_width, 3, 3, group_width)
    same_group = jnp.eye(group_count, dtype=jnp.float32)
    wide = jnp.einsum("gokwc,hg->khcwgo", split, same_group)
    chan_count = group_count * group_width
    return wide.reshape(3, chan_count, 3 * chan_count).astype(jnp.bfloat16)


def grouped_conv(row_above, centre, row_below, kernel, offset_bias, kernel_spacing):
    chan_count = centre.shape[3]
    wide = block_kernels(kernel)
    total = None
    for kh_index, source in enumerate((row_above, centre, row_below)):
        product = jnp.einsum(
            "trwc,ck->trwk", source, wide[kh_index], preferred_element_type=jnp.float32
        )
        for kw_index, offset in enumerate((-kernel_spacing, 0, kernel_spacing)):
            part = product[..., kw_index * chan_count : (kw_index + 1) * chan_count]
            moved = column_view(part, offset)
            total = moved if total is None else total + moved
    summed = total + offset_bias
    return jax.nn.gelu(summed, approximate=False).astype(jnp.bfloat16)


def on_device(feature_map, conv_weight, branch_bias, unite_weight):
    rows_here = feature_map.shape[1]
    distances = (1, 2, 4)
    neighbours = []
    for distance in distances:
        row_above = from_behind(feature_map, "row", distance)
        row_below = from_behind(feature_map, "row", -distance)
        neighbours.append((row_above, row_below))
    branches = []
    for arm_index, distance in enumerate(distances):
        row_above, row_below = neighbours[arm_index]
        branches.append(
            grouped_conv(
                row_above,
                feature_map,
                row_below,
                conv_weight[arm_index],
                branch_bias[arm_index],
                distance * rows_here,
            )
        )
    partial_terms = jnp.dot(branches[0], unite_weight[0], preferred_element_type=jnp.float32)
    for arm_index in (1, 2):
        partial_terms = partial_terms + jnp.dot(
            branches[arm_index], unite_weight[arm_index], preferred_element_type=jnp.float32
        )
    result = lax.psum_scatter(partial_terms, "tp", scatter_dimension=2, tiled=True)
    return result.astype(jnp.bfloat16)


def solution(mesh):
    placed = (
        P(None, "row", None, "tp"),
        P(None, "tp", None, None),
        P(None, "tp"),
        P(None, "tp", None),
    )
    return jax.shard_map(
        on_device, mesh=mesh, in_specs=placed, out_specs=P(None, "row", "tp", None), check_vma=False
    )
```

profile of v0, /device:TPU:6, one launch (start us, length us, event | category | flops | bytes accessed | tf_op | source)
XLA Modules:
  0.0 218.1 jit_solution(16489307111509391203)
XLA Ops:
  6.5 6.0 %collective-permute-start.2 = (bf16[1,8,128,256]{3,2,1,0:T(8,128)(2,1)}, bf16[1,8,128,256]{3,2,1,0:T(8,128)(2,1)}, u32[]{:S(2)}, u32[]{:S(2)}) collective-permute-start(bf16[1,8,128,256]{3,2,1,0:T(8,128)(2,1)} %param.4), channel_id=1, source_target_pairs={{0,32},{16,48},{32,64},{48,80},{64,96},{80,112},{96,128},{112,144}... | collective-permute-start | bytes 1572872 | tf_op jit(solution)/shard_map/ppermute | solution.py:10
  12.5 1.3 collective-permute-start.3
  13.8 4.6 %collective-permute-start = (bf16[1,8,128,256]{3,2,1,0:T(8,128)(2,1)}, bf16[1,8,128,256]{3,2,1,0:T(8,128)(2,1)}, u32[]{:S(2)}, u32[]{:S(2)}) collective-permute-start(bf16[1,8,128,256]{3,2,1,0:T(8,128)(2,1)} %param.4), channel_id=1, source_target_pairs={{0,16},{16,32},{32,48},{48,64},{64,80},{80,96},{96,112},{112,128},... | collective-permute-start | bytes 1572872 | tf_op jit(solution)/shard_map/ppermute | solution.py:10
  18.4 1.3 collective-permute-start.1
  19.7 1.3 collective-permute-start.5
  21.0 1.3 fusion.215
  22.3 0.3 copy.15
  22.6 0.5 copy.11
  23.0 0.3 copy.16
  23.4 1.5 copy.13
  24.8 0.3 copy.14
  25.1 0.5 copy.9
  25.6 5.2 %fusion.2 = (bf16[3,4,64,3,4,64]{5,4,3,2,1,0:T(4,128)(2,1)S(1)}, bf16[3,4,64,3,4,64]{5,4,3,2,1,0:T(4,128)(2,1)S(1)}, bf16[3,4,64,3,4,64]{5,4,3,2,1,0:T(4,128)(2,1)S(1)}) fusion(f32[4,64,3,3,64]{1,0,3,4,2:T(4,128)} %copy.13, f32[4,4]{0,1:T(4,128)S(1)} %convert_bitcast_fusion, f32[4,64,3,3,64]{1,0,3,4,2:T(4,128)S(1)} %copy.11, f32[4,64,3,3,64]{1,0,3,4,2:T(4,128)S(1)} %copy.9), kind=kLoop, calls=%fused_computation.6 | loop fusion | flops 3538944 | bytes 5308480 | tf_op jit(solution)/shard_map/convert_element_type | solution.py:27
  30.8 2.8 %fusion.212 = (bf16[1,4,64,3,4,64]{5,4,3,2,1,0:T(4,128)(2,1)}, bf16[1,4,64,3,4,64]{5,4,3,2,1,0:T(4,128)(2,1)}, bf16[1,4,64,3,4,64]{5,4,3,2,1,0:T(4,128)(2,1)}, b...) fusion(bf16[3,4,64,3,4,64]{5,4,3,2,1,0:T(4,128)(2,1)S(1)} %get-, ...), kind=kLoop, calls=%fused_computation.269 | loop fusion | bytes 4718592 | tf_op jit(solution)/shard_map/slice | solution.py:36
  33.6 1.9 reshape.118
  35.5 0.6 convolution_bitcast_fusion.4
  36.1 1.6 copy-done.1
  37.8 1.5 fusion.207
  39.3 2.1 fusion.214
  41.3 1.9 reshape.114
  43.3 0.6 convolution_bitcast_fusion.7
  43.9 1.6 copy-done
  45.5 1.5 fusion.210
  47.0 0.5 reshape.122
  47.4 1.6 convolution_bitcast_fusion.1
  49.1 1.6 fusion.204
  50.7 2.5 %reshape.117 = bf16[256,768,1]{1,0,2:T(8,128)(2,1)} reshape(bf16[1,4,64,3,4,64]{5,4,3,2,1,0:T(4,128)(2,1)} %get-tuple-element.43) | data formatting | bytes 786432 | tf_op jit(solution)/shard_map/squeeze | solution.py:36
  53.2 2.5 %reshape.119 = bf16[256,768,1]{1,0,2:T(8,128)(2,1)} reshape(bf16[1,4,64,3,4,64]{5,4,3,2,1,0:T(4,128)(2,1)} %get-tuple-element.42) | data formatting | bytes 786432 | tf_op jit(solution)/shard_map/squeeze | solution.py:36
  55.7 2.5 %reshape.113 = bf16[256,768,1]{1,0,2:T(8,128)(2,1)} reshape(bf16[1,4,64,3,4,64]{5,4,3,2,1,0:T(4,128)(2,1)} %get-tuple-element.29) | data formatting | bytes 786432 | tf_op jit(solution)/shard_map/squeeze | solution.py:36
  58.2 2.5 %reshape.115 = bf16[256,768,1]{1,0,2:T(8,128)(2,1)} reshape(bf16[1,4,64,3,4,64]{5,4,3,2,1,0:T(4,128)(2,1)} %get-tuple-element.30) | data formatting | bytes 786432 | tf_op jit(solution)/shard_map/squeeze | solution.py:36
  60.7 2.5 %reshape.123 = bf16[256,768,1]{1,0,2:T(8,128)(2,1)} reshape(bf16[1,4,64,3,4,64]{5,4,3,2,1,0:T(4,128)(2,1)} %get-tuple-element.24) | data formatting | bytes 786432 | tf_op jit(solution)/shard_map/squeeze | solution.py:36
  63.2 1.9 reshape.121
  65.1 12.0 %collective-permute-start.4 = (bf16[1,8,128,256]{3,2,1,0:T(8,128)(2,1)}, bf16[1,8,128,256]{3,2,1,0:T(8,128)(2,1)S(1)}, u32[]{:S(2)}, u32[]{:S(2)}) collective-permute-start(bf16[1,8,128,256]{3,2,1,0:T(8,128)(2,1)} %param.4), channel_id=1, source_target_pairs={{0,64},{16,80},{32,96},{48,112},{64,128},{80,144},{96,160},{112,17... | collective-permute-start | bytes 1572872 | tf_op jit(solution)/shard_map/ppermute | solution.py:10
  77.1 1.7 convolution_bitcast_fusion.5
  78.9 0.2 fusion.206
  79.1 1.7 convolution_bitcast_fusion.3
  80.8 0.2 fusion.208
  81.0 1.7 convolution_bitcast_fusion.8
  82.7 0.2 fusion.209
  82.9 1.7 convolution_bitcast_fusion.6
  84.8 1.6 convolution_bitcast_fusion
  86.6 12.0 %collective-permute-done.4 = bf16[1,8,128,256]{3,2,1,0:T(8,128)(2,1)S(1)} collective-permute-done((bf16[1,8,128,256]{3,2,1,0:T(8,128)(2,1)}, bf16[1,8,128,256]{3,2,1,0:T(8,128)(2,1)S(1)}, u32[]{:S(2)}, u32[]{:S(2)}) %collective-permute-start.4) | collective-permute-done | bytes 524320 | tf_op jit(solution)/shard_map/ppermute | solution.py:10
  98.7 0.6 convolution_bitcast_fusion.2
  99.5 6.3 %fusion.64 = f32[8,128,1024]{2,1,0:T(8,128)} fusion(bf16[3,256,1024]{2,1,0:T(8,128)(2,1)S(1)} %copy-done.15, f32[1,8,128,256]{3,2,1,0:T(8,128)S(1)} %get-tuple-element.16, f32[1,8,128,768]{3,2,1,0:T(8,128)S(1)} %convolution_bitcast_fusion.3, f32[1,8,128,256]{3,2,1,0:T(8,128)S(1)} %get-tuple-element.15, f32[1,8,128,256]{3,2,1,0:T(8,128)S(1)} %copy-done.13, ...), kind=kOutput, calls=%fused_computation.122 | convolution fusion | flops 556269568 | bytes 14156800 | tf_op jit(solution)/shard_map/dot_general | solution.py:69
  105.8 6.4 %fusion.69 = f32[8,128,1024]{2,1,0:T(8,128)} fusion(bf16[3,256,1024]{2,1,0:T(8,128)(2,1)S(1)} %copy-done.15, f32[1,8,128,256]{3,2,1,0:T(8,128)S(1)} %get-tuple-element.22, f32[1,8,128,768]{3,2,1,0:T(8,128)S(1)} %convolution_bitcast_fusion.6, f32[1,8,128,256]{3,2,1,0:T(8,128)S(1)} %get-tuple-element.21, f32[1,8,128,256]{3,2,1,0:T(8,128)S(1)} %copy-done.11, ...), kind=kOutput, calls=%fused_computation.127 | convolution fusion | flops 556269568 | bytes 14156800 | tf_op jit(solution)/shard_map/dot_general | solution.py:67
  112.3 6.9 %add_bitcast_fusion = f32[1,8,128,1024]{3,2,1,0:T(8,128)} fusion(f32[8,128,1024]{2,1,0:T(8,128)} %fusion.69, f32[8,128,1024]{2,1,0:T(8,128)} %fusion.64, bf16[3,256,1024]{2,1,0:T(8,128)(2,1)S(1)} %copy-done.15, f32[1,8,128,256]{3,2,1,0:T(8,128)S(1)} %get-tuple-element.10, f32[1,8,128,768]{3,2,1,0:T(8,128)S(1)} %convolution_bitcast_fusion, ...), kind=kOutput, calls=%fused_computation.3 | convolution fusion | flops 558366720 | bytes 22545408 | tf_op jit(solution)/shard_map/dot_general | solution.py:69
  119.2 90.3 %reduce-scatter.2.cloned.1.call-done = f32[1,8,8,1024]{3,2,1,0:T(8,128)} async-done(((f32[1,8,128,1024]{3,2,1,0:T(8,128)}), f32[1,8,8,1024]{3,2,1,0:T(8,128)}) %reduce-scatter.2.cloned.1.call-update) | async-done | bytes 262160 | tf_op jit(solution)/shard_map/reduce_scatter | solution.py:72
  209.6 1.6 convert_element_type.69
  (42 shorter events, 0.7 us)
Async XLA Ops:
  6.5 203.1 %reduce-scatter.2.cloned.1.call-start = ((), (), s32[]{:S(2)}) async-start(), calls=%async_computation.1 | async-start | bytes 4456448 | tf_op jit(solution)/shard_map/reduce_scatter | solution.py:72
  6.5 58.6 %collective-permute-start.2 = (bf16[1,8,128,256]{3,2,1,0:T(8,128)(2,1)}, bf16[1,8,128,256]{3,2,1,0:T(8,128)(2,1)}, u32[]{:S(2)}, u32[]{:S(2)}) collective-permute-start(bf16[1,8,128,256]{3,2,1,0:T(8,128)(2,1)} %param.4), channel_id=1, source_target_pairs={{0,32},{16,48},{32,64},{48,80},{64,96},{80,112},{96,128},{112,144}... | collective-permute-start | bytes 1572872 | tf_op jit(solution)/shard_map/ppermute | solution.py:10
  12.5 66.6 %collective-permute-start.3 = (bf16[1,8,128,256]{3,2,1,0:T(8,128)(2,1)}, bf16[1,8,128,256]{3,2,1,0:T(8,128)(2,1)}, u32[]{:S(2)}, u32[]{:S(2)}) collective-permute-start(bf16[1,8,128,256]{3,2,1,0:T(8,128)(2,1)} %param.4), channel_id=1, source_target_pairs={{32,0},{48,16},{64,32},{80,48},{96,64},{112,80},{128,96},{144,112}... | collective-permute-start | bytes 1572872 | tf_op jit(solution)/shard_map/ppermute | solution.py:10
  13.8 67.2 %collective-permute-start = (bf16[1,8,128,256]{3,2,1,0:T(8,128)(2,1)}, bf16[1,8,128,256]{3,2,1,0:T(8,128)(2,1)}, u32[]{:S(2)}, u32[]{:S(2)}) collective-permute-start(bf16[1,8,128,256]{3,2,1,0:T(8,128)(2,1)} %param.4), channel_id=1, source_target_pairs={{0,16},{16,32},{32,48},{48,64},{64,80},{80,96},{96,112},{112,128},... | collective-permute-start | bytes 1572872 | tf_op jit(solution)/shard_map/ppermute | solution.py:10
  18.4 64.5 %collective-permute-start.1 = (bf16[1,8,128,256]{3,2,1,0:T(8,128)(2,1)}, bf16[1,8,128,256]{3,2,1,0:T(8,128)(2,1)}, u32[]{:S(2)}, u32[]{:S(2)}) collective-permute-start(bf16[1,8,128,256]{3,2,1,0:T(8,128)(2,1)} %param.4), channel_id=1, source_target_pairs={{16,0},{32,16},{48,32},{64,48},{80,64},{96,80},{112,96},{128,112},... | collective-permute-start | bytes 1572872 | tf_op jit(solution)/shard_map/ppermute | solution.py:10
  19.7 65.1 %collective-permute-start.5 = (bf16[1,8,128,256]{3,2,1,0:T(8,128)(2,1)}, bf16[1,8,128,256]{3,2,1,0:T(8,128)(2,1)}, u32[]{:S(2)}, u32[]{:S(2)}) collective-permute-start(bf16[1,8,128,256]{3,2,1,0:T(8,128)(2,1)} %param.4), channel_id=1, source_target_pairs={{64,0},{80,16},{96,32},{112,48},{128,64},{144,80},{160,96},{176,11... | collective-permute-start | bytes 1572872 | tf_op jit(solution)/shard_map/ppermute | solution.py:10
  30.8 4.7 %copy-start.2 = (bf16[1,8,128,256]{3,2,1,0:T(8,128)(2,1)S(1)}, bf16[1,8,128,256]{3,2,1,0:T(8,128)(2,1)}, u32[]{:S(2)}) copy-start(bf16[1,8,128,256]{3,2,1,0:T(8,128)(2,1)} %param.4) | copy-start | bytes 1572868
  36.1 1.7 copy-start.1
  43.3 3.7 %copy-start.3 = (bf16[1,4,64,3,4,64]{5,4,3,2,1,0:T(4,128)(2,1)S(1)}, bf16[1,4,64,3,4,64]{5,4,3,2,1,0:T(4,128)(2,1)}, u32[]{:S(2)}) copy-start(bf16[1,4,64,3,4,64]{5,4,3,2,1,0:T(4,128)(2,1)} %get-tuple-element.25) | copy-start | bytes 1179652
  43.8 1.6 copy-start
  47.4 3.2 %copy-start.14 = (f32[3,256]{1,0:T(4,128)S(1)}, f32[3,256]{1,0:T(4,128)}, u32[]{:S(2)}) copy-start(f32[3,256]{1,0:T(4,128)} %param.6) | copy-start | bytes 9220
  65.1 14.0 %copy-start.7 = (bf16[256,768,1]{1,0,2:T(8,128)(2,1)S(1)}, bf16[256,768,1]{1,0,2:T(8,128)(2,1)}, u32[]{:S(2)}) copy-start(bf16[256,768,1]{1,0,2:T(8,128)(2,1)} %reshape.119) | copy-start | bytes 1179652
  65.1 33.5 %collective-permute-start.4 = (bf16[1,8,128,256]{3,2,1,0:T(8,128)(2,1)}, bf16[1,8,128,256]{3,2,1,0:T(8,128)(2,1)S(1)}, u32[]{:S(2)}, u32[]{:S(2)}) collective-permute-start(bf16[1,8,128,256]{3,2,1,0:T(8,128)(2,1)} %param.4), channel_id=1, source_target_pairs={{0,64},{16,80},{32,96},{48,112},{64,128},{80,144},{96,160},{112,17... | collective-permute-start | bytes 1572872 | tf_op jit(solution)/shard_map/ppermute | solution.py:10
  79.1 1.9 copy-start.6
  81.0 1.9 copy-start.5
  82.9 1.9 copy-start.4
  86.6 12.8 %copy-start.12 = (f32[1,8,128,256]{3,2,1,0:T(8,128)S(1)}, f32[1,8,128,256]{3,2,1,0:T(8,128)}, u32[]{:S(2)}) copy-start(f32[1,8,128,256]{3,2,1,0:T(8,128)} %get-tuple-element.13) | copy-start | bytes 3145732
  86.6 12.8 %copy-start.13 = (f32[1,8,128,256]{3,2,1,0:T(8,128)S(1)}, f32[1,8,128,256]{3,2,1,0:T(8,128)}, u32[]{:S(2)}) copy-start(f32[1,8,128,256]{3,2,1,0:T(8,128)} %get-tuple-element.14) | copy-start | bytes 3145732
  86.6 12.8 %copy-start.15 = (bf16[3,256,1024]{2,1,0:T(8,128)(2,1)S(1)}, bf16[3,256,1024]{2,1,0:T(8,128)(2,1)}, u32[]{:S(2)}) copy-start(bf16[3,256,1024]{2,1,0:T(8,128)(2,1)} %param.7) | copy-start | bytes 4718596
  99.5 6.4 %copy-start.10 = (f32[1,8,128,256]{3,2,1,0:T(8,128)S(1)}, f32[1,8,128,256]{3,2,1,0:T(8,128)}, u32[]{:S(2)}) copy-start(f32[1,8,128,256]{3,2,1,0:T(8,128)} %get-tuple-element.19) | copy-start | bytes 3145732
  99.5 6.4 %copy-start.11 = (f32[1,8,128,256]{3,2,1,0:T(8,128)S(1)}, f32[1,8,128,256]{3,2,1,0:T(8,128)}, u32[]{:S(2)}) copy-start(f32[1,8,128,256]{3,2,1,0:T(8,128)} %get-tuple-element.20) | copy-start | bytes 3145732
  105.8 6.4 %copy-start.8 = (f32[1,8,128,256]{3,2,1,0:T(8,128)S(1)}, f32[1,8,128,256]{3,2,1,0:T(8,128)}, u32[]{:S(2)}) copy-start(f32[1,8,128,256]{3,2,1,0:T(8,128)} %get-tuple-element.7) | copy-start | bytes 3145732
  105.8 6.4 %copy-start.9 = (f32[1,8,128,256]{3,2,1,0:T(8,128)S(1)}, f32[1,8,128,256]{3,2,1,0:T(8,128)}, u32[]{:S(2)}) copy-start(f32[1,8,128,256]{3,2,1,0:T(8,128)} %get-tuple-element.8) | copy-start | bytes 3145732
Sparse Core Ops, SparseCore 0:
  119.4 90.1 reduce-scatter.1
where the time goes:
time: 219 us; the launch traced here: 218 us
  waiting for transfers between devices  102 us (47%)
  local copies, waits for them, and re-layouts  37.2 us (17%)
  matrix products  31.5 us (14%)
  starting transfers between devices  26.4 us (12%)
  between operations  13.8 us (6%)
  other arithmetic  6.78 us (3%)
    reduce_scatter x1, waiting for transfers between devices, on_device(): lax.psum_scatter(partial_terms, 'tp', scatter_dimension=2, tiled=True)  90.3 us
    ppermute x6, starting transfers between devices, from_behind(): return lax.ppermute(array, axis, pairs)  26.4 us
    squeeze x9, local copies, waits for them, and re-layouts, grouped_conv(): wide[kh_index]  18.7 us
    dot_general x2, matrix products, on_device(): jnp.dot(branches[arm_index], unite_weight[arm_index], preferred_element_t...  13.3 us
    ppermute x6, waiting for transfers between devices, from_behind(): return lax.ppermute(array, axis, pairs)  12 us
    dot_general x9, matrix products, grouped_conv(): jnp.einsum('trwc,ck->trwk', source, wide[kh_index], preferred_element_typ...  11.7 us
    dot_general x1, matrix products, on_device(): jnp.dot(branches[0], unite_weight[0], preferred_element_type=jnp.float32)  6.43 us
    slice x9, local copies, waits for them, and re-layouts, grouped_conv(): part = product[..., kw_index * chan_count:(kw_index + 1) * chan_count]  5.72 us
  transfers between devices with their start and end apart: 7, of which 2 were waited for; matrix products, arithmetic and copies ran while one was open for 23% of the time, Pallas kernels for 0%

commit v1 on v0

v1 whole, which is shorter than its diff:
```python
import jax
import jax.numpy as jnp
from jax import lax
from jax.experimental import pallas as pl
from jax.experimental.pallas import tpu as pltpu
from jax.sharding import PartitionSpec as P


DISTANCES = (1, 2, 4)
BANDS = 16
SPOTS = 16
LOW = 4
PIXELS = BANDS * LOW
PAD = 4
TAPS = 9


def swap_halves(even, odd):
    low = lax.broadcasted_iota(jnp.int32, even.shape, even.ndim - 2) < LOW
    axis = even.ndim - 2
    first = jnp.where(low, even, pltpu.roll(odd, LOW, axis))
    second = jnp.where(low, pltpu.roll(even, LOW, axis), odd)
    return first, second


def pack_kernel(x_ref, out_ref):
    chan = x_ref.shape[2]
    for j in range(8):
        v = x_ref[j].astype(jnp.float32).reshape(8, 2, 8, chan)
        first, second = swap_halves(v[:, 0], v[:, 1])
        out_ref[j] = first.reshape(PIXELS, chan).astype(jnp.bfloat16)
        out_ref[8 + j] = second.reshape(PIXELS, chan).astype(jnp.bfloat16)


def pack(x):
    return pl.pallas_call(
        pack_kernel,
        out_shape=jax.ShapeDtypeStruct((16, PIXELS, x.shape[2]), jnp.bfloat16),
        name="pack",
    )(x)


def widen_kernel(w_ref, out_ref):
    chan = w_ref.shape[1]
    rows = lax.broadcasted_iota(jnp.int32, (chan, chan), 0) // 64
    cols = lax.broadcasted_iota(jnp.int32, (chan, chan), 1) // 64
    same = rows == cols
    for tap in range(TAPS):
        start, width = (tap // 2) * 128, 128 if tap < 8 else 64
        shift = (tap % 2) * 64
        place = lax.broadcasted_iota(jnp.int32, (chan, width), 0) % 64 + shift
        pick = (place == lax.broadcasted_iota(jnp.int32, (chan, width), 1)).astype(jnp.float32).astype(jnp.bfloat16)
        for arm in range(3):
            slab = w_ref[arm, :, start : start + width]
            wide = lax.dot_general(pick, slab, (((1,), (1,)), ((), ())), preferred_element_type=jnp.float32)
            out_ref[arm, tap * chan : (tap + 1) * chan, :] = jnp.where(same, wide, 0.0).astype(jnp.bfloat16)


def widen(conv_weight):
    chan = conv_weight.shape[1] * conv_weight.shape[2]
    return pl.pallas_call(
        widen_kernel,
        out_shape=jax.ShapeDtypeStruct((3, TAPS * chan, chan), jnp.bfloat16),
        name="widen",
    )(conv_weight.reshape(3, chan, -1))


def shifted(v, by):
    chan = v.shape[1]
    row = lax.broadcasted_iota(jnp.int32, v.shape, 0)
    if by == 0:
        return v
    if by == LOW:
        return jnp.where(row >= LOW, pltpu.roll(v, LOW, 0), 0.0)
    if by == -LOW:
        return jnp.where(row < PIXELS - LOW, pltpu.roll(v, PIXELS - LOW, 0), 0.0)
    zeros = jnp.zeros((abs(by), chan), v.dtype)
    if by > 0:
        return jnp.concatenate([zeros, v[: PIXELS - by]], axis=0)
    return jnp.concatenate([v[-by:], zeros], axis=0)


SHIFTS = (0, 1, -1, 2, -2, 4, -4)


def head_kernel(core_ref, x_ref, w_ref, bias_ref, unite_ref, send_ref, keep_ref, s_ref):
    step = pl.program_id(0)
    chan = x_ref.shape[2]

    @pl.when(step == 0)
    def _():
        zeros = jnp.zeros((len(SHIFTS), PAD, PIXELS, chan), jnp.bfloat16)
        s_ref[:, :PAD] = zeros
        s_ref[:, PAD + SPOTS :] = zeros
        for quad in range(4):
            v = x_ref[:, quad * 16 : (quad + 1) * 16, :].astype(jnp.float32).reshape(8, 2, 2, 8, chan)
            halves = swap_halves(v[:, 0], v[:, 1])
            for pair in range(2):
                for side in range(2):
                    spot = PAD + 4 * quad + 2 * pair + side
                    mine = halves[side][:, pair].reshape(PIXELS, chan)
                    for at, shift in enumerate(SHIFTS):
                        s_ref[at, spot] = shifted(mine, LOW * shift).astype(jnp.bfloat16)

    core = core_ref[0]
    spots = [PAD + 4 * step + 2 * half + (side + core) % 2 for side in (1, 0) for half in (0, 1)]
    hidden = []
    for arm, distance in enumerate(DISTANCES):
        total = None
        for kh in range(3):
            at = SHIFTS.index((1 - kh) * distance)
            for kw in range(3):
                left = jnp.concatenate([s_ref[at, spot + (kw - 1) * distance] for spot in spots], axis=0)
                tap = 3 * kh + kw
                part = jnp.dot(left, w_ref[arm, tap * chan : (tap + 1) * chan, :], preferred_element_type=jnp.float32)
                total = part if total is None else total + part
        summed = total + bias_ref[arm : arm + 1, :]
        hidden.append((0.5 * summed * (1.0 + lax.erf(summed * (0.5**0.5)))).astype(jnp.bfloat16))
    term = None
    for arm in range(3):
        part = jnp.dot(hidden[arm], unite_ref[arm], preferred_element_type=jnp.float32)
        term = part if term is None else term + part
    term = term.astype(jnp.bfloat16).reshape(4, PIXELS, -1)
    send_ref[...] = term[:2]
    keep_ref[...] = term[2:]


def head_terms(core, x, wide, bias, unite):
    chan, width = x.shape[2], unite.shape[2]
    whole = lambda *dims: pl.BlockSpec(dims, lambda step, core: (0,) * len(dims))
    out = jax.ShapeDtypeStruct((8, PIXELS, width), jnp.bfloat16)
    out_spec = pl.BlockSpec((2, PIXELS, width), lambda step, core: (step, 0, 0))
    return pl.pallas_call(
        head_kernel,
        grid_spec=pltpu.PrefetchScalarGridSpec(
            num_scalar_prefetch=1,
            grid=(4,),
            in_specs=[whole(*x.shape), whole(*wide.shape), whole(*bias.shape), whole(*unite.shape)],
            out_specs=[out_spec, out_spec],
            scratch_shapes=[pltpu.VMEM((len(SHIFTS), SPOTS + 2 * PAD, PIXELS, chan), jnp.bfloat16)],
        ),
        out_shape=[out, out],
        compiler_params=pltpu.CompilerParams(vmem_limit_bytes=48 * 2**20),
        cost_estimate=pl.CostEstimate(flops=5 * 10**9, bytes_accessed=8 * 10**6, transcendentals=10**6),
        name="head",
    )(core, x, wide, bias, unite)


def on_device(feature_map, conv_weight, branch_bias, unite_weight):
    core = (lax.axis_index("tp") % 2).astype(jnp.int32).reshape(1)
    packed = pack(feature_map[0])
    wide = widen(conv_weight)
    mine = lax.all_to_all(packed, "row", 0, 0)
    send, keep = head_terms(core, mine, wide, branch_bias, unite_weight)
    other = lax.ppermute(send, "tp", [(i, i ^ 1) for i in range(16)])
    both = (keep.astype(jnp.float32) + other.astype(jnp.float32)).astype(jnp.bfloat16)
    chips = [[core_at + 2 * chip for chip in range(8)] for core_at in range(2)]
    terms = lax.all_to_all(both, "tp", 0, 0, axis_index_groups=chips)
    result = jnp.sum(terms.astype(jnp.float32), axis=0).astype(jnp.bfloat16)
    bands = lax.all_to_all(result.reshape(BANDS, LOW, -1), "row", 0, 0)
    width = bands.shape[2]
    return bands.reshape(2, 8, LOW, width).transpose(1, 0, 2, 3).reshape(1, 8, 8, width)


def solution(mesh):
    placed = (
        P(None, "row", None, "tp"),
        P(None, "tp", None, None),
        P(None, "tp"),
        P(None, "tp", None),
    )
    return jax.shard_map(
        on_device, mesh=mesh, in_specs=placed, out_specs=P(None, "row", "tp", None), check_vma=False
    )
```

time: 219 us -> 77.1 us (0.35)
  waiting for transfers between devices: 102 us -> 14.2 us
  local copies, waits for them, and re-layouts: 37.2 us -> 0.86 us
  blocking collectives: 0 us -> 34.4 us
  matrix products: 31.5 us -> 0 us
  starting transfers between devices: 26.4 us -> 9.67 us
  Pallas kernels: 0 us -> 15.8 us
  between operations: 13.8 us -> 0.08 us
  other arithmetic: 6.78 us -> 0.58 us
    reduce_scatter x1 -> x0, waiting for transfers between devices: 90.3 us -> none  [on_device(): lax.psum_scatter(partial_terms, 'tp', scatter_dimension=2, tiled=True)]
    all_to_all x0 -> x2, blocking collectives: none -> 34.4 us  [the longest x1 21.9 us: on_device(): terms = lax.all_to_all(both, 'tp', 0, 0, axis_index_groups=chips)]
    dot_general x12 -> x0, matrix products: 31.5 us -> none  [the longest x2 13.3 us: on_device(): jnp.dot(branches[arm_index], unite_weight[arm_index], preferred_element_t...]
    ppermute x6 -> x1, starting transfers between devices: 26.4 us -> 0.09 us  [on_device(): other = lax.ppermute(send, 'tp', [(i, i ^ 1) for i in range(16)])]
    squeeze x9 -> x0, local copies, waits for them, and re-layouts: 18.7 us -> none  [grouped_conv(): wide[kh_index]]
    pallas_call x0 -> x3, Pallas kernels: none -> 15.8 us  [the longest x1 9.73 us: head_terms(): pl.pallas_call(head_kernel, grid_spec=pltpu.PrefetchScalarGridSpec(num_sc...]
    slice x13 -> x0, local copies, waits for them, and re-layouts: 11.9 us -> none  [the longest x9 5.72 us: grouped_conv(): part = product[..., kw_index * chan_count:(kw_index + 1) * chan_count]]
    all_to_all x0 -> x1, waiting for transfers between devices: none -> 11.5 us  [on_device(): mine = lax.all_to_all(packed, 'row', 0, 0)]
  transfers between devices with their start and end apart: 7 -> 2, of which waited for: 2 -> 2; matrix products, arithmetic and copies ran while one was open for 23% -> 0% of each run, Pallas kernels for 0% -> 5%
where the time goes in v1:
time: 77.1 us; the launch traced here: 75.6 us
  blocking collectives  34.4 us (45%)
  Pallas kernels  15.8 us (20%)
  waiting for transfers between devices  14.2 us (18%)
  starting transfers between devices  9.67 us (13%)
  local copies, waits for them, and re-layouts  0.86 us (1%)
    all_to_all x1, blocking collectives, on_device(): terms = lax.all_to_all(both, 'tp', 0, 0, axis_index_groups=chips)  21.9 us
    all_to_all x1, blocking collectives, on_device(): bands = lax.all_to_all(result.reshape(BANDS, LOW, -1), 'row', 0, 0)  12.6 us
    all_to_all x1, waiting for transfers between devices, on_device(): mine = lax.all_to_all(packed, 'row', 0, 0)  11.5 us
    pallas_call x1, Pallas kernels, head_terms(): pl.pallas_call(head_kernel, grid_spec=pltpu.PrefetchScalarGridSpec(num_sc...  9.73 us
    all_to_all x1, starting transfers between devices, on_device(): mine = lax.all_to_all(packed, 'row', 0, 0)  9.58 us
    pallas_call x1, Pallas kernels, widen(): pl.pallas_call(widen_kernel, out_shape=jax.ShapeDtypeStruct((3, TAPS * ch...  4.15 us
    ppermute x1, waiting for transfers between devices, on_device(): other = lax.ppermute(send, 'tp', [(i, i ^ 1) for i in range(16)])  2.65 us
    pallas_call x1, Pallas kernels, pack(): pl.pallas_call(pack_kernel, out_shape=jax.ShapeDtypeStruct((16, PIXELS, x...  1.96 us
  transfers between devices with their start and end apart: 2, of which 2 were waited for; matrix products, arithmetic and copies ran while one was open for 0% of the time, Pallas kernels for 5%

profile of v1, /device:TPU:6, one launch (start us, length us, event | category | flops | bytes accessed | tf_op | source)
XLA Modules:
  0.0 75.6 jit_solution(12460956027776027331)
XLA Ops:
  0.0 2.0 %pack.1 = bf16[16,64,256]{2,1,0:T(8,128)(2,1)} custom-call(bf16[8,128,256]{2,1,0:T(8,128)(2,1)} %bitcast.10), custom_call_target="tpu_custom_call" | custom-call | tf_op jit(solution)/shard_map/pack/pallas_call | solution.py:36
  2.0 9.6 %all-to-all-start = ((bf16[16,64,256]{2,1,0:T(8,128)(2,1)}), bf16[16,64,256]{2,1,0:T(8,128)(2,1)S(1)}, u32[]{:S(2)}, u32[]{:S(2)}) async-start(bf16[16,64,256]{2,1,0:T(8,128)(2,1)} %pack.1), calls=%async_computation | async-start | bytes 1048576 | tf_op jit(solution)/shard_map/all_to_all | solution.py:153
  11.6 0.0 copy-start
  11.6 0.0 copy-start.1
  11.6 4.2 %widen.1.w_ref = bf16[3,2304,256]{2,1,0:T(8,128)(2,1)} custom-call(bf16[3,256,576]{2,1,0:T(8,128)(2,1)} %bitcast.9), custom_call_target="tpu_custom_call" | custom-call | tf_op jit(solution)/shard_map/widen/pallas_call | solution.py:61
  15.7 11.5 %all-to-all-done.x_ref = bf16[16,64,256]{2,1,0:T(8,128)(2,1)S(1)} async-done(((bf16[16,64,256]{2,1,0:T(8,128)(2,1)}), bf16[16,64,256]{2,1,0:T(8,128)(2,1)S(1)}, u32[]{:S(2)}, u32[]{:S(2)}) %all-to-all-start) | async-done | bytes 524320 | tf_op jit(solution)/shard_map/all_to_all | solution.py:153
  27.2 0.0 copy-done
  27.2 0.0 copy-done.1
  27.2 9.7 %head.1 = (bf16[8,64,1024]{2,1,0:T(8,128)(2,1)S(1)}, bf16[8,64,1024]{2,1,0:T(8,128)(2,1)S(1)}) custom-call(s32[1]{0:T(128)} %bitcast.core_ref, bf16[16,64,256]{2,1,0:T(8,128)(2,1)S(1)} %all-to-all-done.x_ref, bf16[3,2304,256]{2,1,0:T(8,128)(2,1)} %widen.1.w_ref, f32[3,256]{1,0:T(4,128)S(1)} %copy-done.1, bf16[3,256,1024]{2,1,0:T(8,128)(2,1)S(1)} %copy-done), custom_call_target="tpu_custom_call" | custom-call | flops 5000000000 | bytes 8000000 | tf_op jit(solution)/shard_map/head/pallas_call | solution.py:133
  37.0 0.1 collective-permute-start
  37.1 2.6 %collective-permute-done = bf16[8,64,1024]{2,1,0:T(8,128)(2,1)S(1)} collective-permute-done((bf16[8,64,1024]{2,1,0:T(8,128)(2,1)S(1)}, bf16[8,64,1024]{2,1,0:T(8,128)(2,1)S(1)}, u32[]{:S(2)}, u32[]{:S(2)}) %collective-permute-start) | collective-permute-done | bytes 1048608 | tf_op jit(solution)/shard_map/ppermute | solution.py:155
  39.7 0.4 add_convert_fusion
  40.1 21.9 %all_to_all.15 = bf16[8,64,1024]{2,1,0:T(8,128)(2,1)S(1)} all-to-all(bf16[8,64,1024]{2,1,0:T(8,128)(2,1)S(1)} %add_convert_fusion), channel_id=1, replica_groups={{0,2,4,6,8,10,12,14},{1,3,5,7,9,11,13,15},{16,18,20,22,24,26,28,30},{17..., dimensions={0} | all-to-all | bytes 2097152 | tf_op jit(solution)/shard_map/all_to_all | solution.py:158
  62.0 0.2 reduce_sum.12
  62.2 0.1 reshape.17
  62.2 12.6 %all_to_all.16 = bf16[16,4,1024]{2,1,0:T(4,128)(2,1)S(1)} all-to-all(bf16[16,4,1024]{2,1,0:T(4,128)(2,1)S(1)} %reshape.17), channel_id=1, replica_groups=mesh['row'=16,'tp'=16] {'row'}, dimensions={0} | all-to-all | bytes 262144 | tf_op jit(solution)/shard_map/all_to_all | solution.py:160
  74.9 0.7 copy.7
  (2 shorter events, 0.1 us)
Async XLA Ops:
  2.0 25.3 %all-to-all-start = ((bf16[16,64,256]{2,1,0:T(8,128)(2,1)}), bf16[16,64,256]{2,1,0:T(8,128)(2,1)S(1)}, u32[]{:S(2)}, u32[]{:S(2)}) async-start(bf16[16,64,256]{2,1,0:T(8,128)(2,1)} %pack.1), calls=%async_computation | async-start | bytes 1048576 | tf_op jit(solution)/shard_map/all_to_all | solution.py:153
  11.6 15.7 %copy-start = (bf16[3,256,1024]{2,1,0:T(8,128)(2,1)S(1)}, bf16[3,256,1024]{2,1,0:T(8,128)(2,1)}, u32[]{:S(2)}) copy-start(bf16[3,256,1024]{2,1,0:T(8,128)(2,1)} %unite_ref.1) | copy-start | bytes 4718596
  11.6 15.7 %copy-start.1 = (f32[3,256]{1,0:T(4,128)S(1)}, f32[3,256]{1,0:T(4,128)}, u32[]{:S(2)}) copy-start(f32[3,256]{1,0:T(4,128)} %bias_ref.1) | copy-start | bytes 9220
  37.0 2.7 %collective-permute-start = (bf16[8,64,1024]{2,1,0:T(8,128)(2,1)S(1)}, bf16[8,64,1024]{2,1,0:T(8,128)(2,1)S(1)}, u32[]{:S(2)}, u32[]{:S(2)}) collective-permute-start(bf16[8,64,1024]{2,1,0:T(8,128)(2,1)S(1)} %get-tuple-element.8), channel_id=1, source_target_pairs={{0,1},{1,0},{2,3},{3,2},{4,5},{5,4},{6,7},{7,6},{8,9},{9,8},{10,11... | collective-permute-start | bytes 3145736 | tf_op jit(solution)/shard_map/ppermute | solution.py:155

commit v2 on v1

v2 whole, which is shorter than its diff:
```python
import functools

import jax
import jax.numpy as jnp
from jax import lax
from jax.experimental import pallas as pl
from jax.experimental.pallas import tpu as pltpu
from jax.sharding import PartitionSpec as P


DISTANCES = (1, 2, 4)
BANDS = 16
SPOTS = 16
LOW = 4
PIXELS = BANDS * LOW
PAD = 4
TAPS = 9
VMEM_SPEC = pl.BlockSpec(memory_space=pltpu.VMEM)


def in_vmem(array):
    return pltpu.with_memory_space_constraint(array, pltpu.VMEM)


def swap_halves(even, odd):
    low = lax.broadcasted_iota(jnp.int32, even.shape, even.ndim - 2) < LOW
    axis = even.ndim - 2
    first = jnp.where(low, even, pltpu.roll(odd, LOW, axis))
    second = jnp.where(low, pltpu.roll(even, LOW, axis), odd)
    return first, second


def pack_kernel(x_ref, out_ref):
    chan = x_ref.shape[2]
    for j in range(8):
        v = x_ref[j].astype(jnp.float32).reshape(8, 2, 8, chan)
        first, second = swap_halves(v[:, 0], v[:, 1])
        out_ref[j] = first.reshape(PIXELS, chan).astype(jnp.bfloat16)
        out_ref[8 + j] = second.reshape(PIXELS, chan).astype(jnp.bfloat16)


def pack(x):
    return pl.pallas_call(
        pack_kernel,
        out_specs=VMEM_SPEC,
        out_shape=pltpu.VMEM((16, PIXELS, x.shape[2]), jnp.bfloat16),
        compiler_params=pltpu.CompilerParams(vmem_limit_bytes=16 * 2**20),
        name="pack",
    )(x)


def widen_kernel(w_ref, out_ref):
    chan = w_ref.shape[1]
    rows = lax.broadcasted_iota(jnp.int32, (chan, chan), 0) // 64
    cols = lax.broadcasted_iota(jnp.int32, (chan, chan), 1) // 64
    same = rows == cols
    for tap in range(TAPS):
        start, width = (tap // 2) * 128, 128 if tap < 8 else 64
        shift = (tap % 2) * 64
        place = lax.broadcasted_iota(jnp.int32, (chan, width), 0) % 64 + shift
        pick = (place == lax.broadcasted_iota(jnp.int32, (chan, width), 1)).astype(jnp.float32).astype(jnp.bfloat16)
        for arm in range(3):
            slab = w_ref[arm, :, start : start + width]
            wide = lax.dot_general(pick, slab, (((1,), (1,)), ((), ())), preferred_element_type=jnp.float32)
            out_ref[arm, tap * chan : (tap + 1) * chan, :] = jnp.where(same, wide, 0.0).astype(jnp.bfloat16)


def widen(conv_weight):
    chan = conv_weight.shape[1] * conv_weight.shape[2]
    return pl.pallas_call(
        widen_kernel,
        out_shape=jax.ShapeDtypeStruct((3, TAPS * chan, chan), jnp.bfloat16),
        compiler_params=pltpu.CompilerParams(vmem_limit_bytes=16 * 2**20),
        name="widen",
    )(conv_weight.reshape(3, chan, -1))


def shifted(v, by):
    chan = v.shape[1]
    row = lax.broadcasted_iota(jnp.int32, v.shape, 0)
    if by == 0:
        return v
    if by == LOW:
        return jnp.where(row >= LOW, pltpu.roll(v, LOW, 0), 0.0)
    if by == -LOW:
        return jnp.where(row < PIXELS - LOW, pltpu.roll(v, PIXELS - LOW, 0), 0.0)
    zeros = jnp.zeros((abs(by), chan), v.dtype)
    if by > 0:
        return jnp.concatenate([zeros, v[: PIXELS - by]], axis=0)
    return jnp.concatenate([v[-by:], zeros], axis=0)


SHIFTS = (0, 1, -1, 2, -2, 4, -4)


def spread_kernel(x_ref, s_ref):
    chan = x_ref.shape[2]
    zeros = jnp.zeros((len(SHIFTS), PAD, PIXELS, chan), jnp.bfloat16)
    s_ref[:, :PAD] = zeros
    s_ref[:, PAD + SPOTS :] = zeros
    for quad in range(4):
        v = x_ref[:, quad * 16 : (quad + 1) * 16, :].astype(jnp.float32).reshape(8, 2, 2, 8, chan)
        halves = swap_halves(v[:, 0], v[:, 1])
        for pair in range(2):
            for side in range(2):
                spot = PAD + 4 * quad + 2 * pair + side
                mine = halves[side][:, pair].reshape(PIXELS, chan)
                for at, shift in enumerate(SHIFTS):
                    s_ref[at, spot] = shifted(mine, LOW * shift).astype(jnp.bfloat16)


def spread(x):
    return pl.pallas_call(
        spread_kernel,
        in_specs=[VMEM_SPEC],
        out_specs=VMEM_SPEC,
        out_shape=pltpu.VMEM((len(SHIFTS), SPOTS + 2 * PAD, PIXELS, x.shape[2]), jnp.bfloat16),
        compiler_params=pltpu.CompilerParams(vmem_limit_bytes=16 * 2**20),
        name="spread",
    )(x)


def added(*terms):
    return sum(term.astype(jnp.float32) for term in terms)


def far_kernel(keep_ref, other_ref, out_ref):
    for at in range(2):
        out_ref[at] = added(keep_ref[at], other_ref[at]).astype(jnp.bfloat16)


def mid_kernel(keep_ref, across_ref, out_ref):
    for at in range(2):
        out_ref[at] = added(keep_ref[at], across_ref[at])


def split_kernel(mid_ref, other_ref, first_ref, second_ref):
    for at, out_ref in enumerate((first_ref, second_ref)):
        out_ref[...] = added(mid_ref[at], other_ref[at]).astype(out_ref.dtype)


def near_kernel(keep_ref, other_ref, across_ref, first_ref, second_ref):
    for at, out_ref in enumerate((first_ref, second_ref)):
        out_ref[...] = added(keep_ref[at], other_ref[at], across_ref[at]).astype(out_ref.dtype)


def call_add(kernel, name, out, *terms):
    return pl.pallas_call(
        kernel,
        in_specs=[VMEM_SPEC] * len(terms),
        out_specs=[VMEM_SPEC] * len(out),
        out_shape=out,
        compiler_params=pltpu.CompilerParams(vmem_limit_bytes=8 * 2**20),
        name=name,
    )(*[in_vmem(term) for term in terms])


def head_kernel(chunk, spot_ref, s_ref, w_ref, bias_ref, unite_ref, *refs):
    send_ref, keep_ref = refs[-2:]
    chan = s_ref.shape[3]
    spots = [PAD + spot_ref[chunk, at] for at in range(4)]
    hidden = []
    for arm, distance in enumerate(DISTANCES):
        total = None
        for kh in range(3):
            at = SHIFTS.index((1 - kh) * distance)
            for kw in range(3):
                left = jnp.concatenate([s_ref[at, spot + (kw - 1) * distance] for spot in spots], axis=0)
                tap = 3 * kh + kw
                part = jnp.dot(left, w_ref[arm, tap * chan : (tap + 1) * chan, :], preferred_element_type=jnp.float32)
                total = part if total is None else total + part
        summed = total + bias_ref[arm : arm + 1, :]
        hidden.append((0.5 * summed * (1.0 + lax.erf(summed * (0.5**0.5)))).astype(jnp.bfloat16))
    term = None
    for arm in range(3):
        part = jnp.dot(hidden[arm], unite_ref[arm], preferred_element_type=jnp.float32)
        term = part if term is None else term + part
    term = term.reshape(4, PIXELS, -1)
    send_ref[...] = term[:2].astype(jnp.bfloat16)
    keep_ref[...] = term[2:]


def head_terms(chunk, spots, spread_x, wide, bias, unite, after):
    out = [pltpu.VMEM((2, PIXELS, unite.shape[2]), dtype) for dtype in (jnp.bfloat16, jnp.float32)]
    return pl.pallas_call(
        functools.partial(head_kernel, chunk),
        in_specs=[pl.BlockSpec(memory_space=pltpu.SMEM)] + [VMEM_SPEC] * 4 + [pl.BlockSpec(memory_space=pl.ANY)] * len(after),
        out_specs=[VMEM_SPEC] * 2,
        out_shape=out,
        compiler_params=pltpu.CompilerParams(vmem_limit_bytes=16 * 2**20),
        name="head",
    )(spots, spread_x, wide, bias, unite, *after)


CHUNKS = (((2, 1), (1, 1)), ((3, 1), (0, 1)), ((2, 0), (1, 0)), ((3, 0), (0, 0)))
SWAP = [(i, i ^ 1) for i in range(16)]
FAR = [(i, i ^ 2) for i in range(16)]


def hop(ahead):
    return [(i, (i + 4 * ahead) % 16) for i in range(16)]


def on_device(feature_map, conv_weight, branch_bias, unite_weight):
    at = lax.axis_index("tp").astype(jnp.int32)
    chip_x, chip_y, core = at // 4, (at // 2) % 2, at % 2
    spots = jnp.stack([
        jnp.stack([4 * ((chip_x + ahead) % 4) + 2 * ((chip_y + across) % 2) + (core + side) % 2 for side in (1, 0) for ahead, across in chunk])
        for chunk in CHUNKS
    ])
    packed = pack(feature_map[0])
    wide = in_vmem(widen(conv_weight))
    mine = lax.all_to_all(packed, "row", 0, 0)
    spread_x = spread(mine)
    unite, bias = in_vmem(unite_weight), in_vmem(branch_bias)
    width = unite_weight.shape[2]
    bf16, f32 = (pltpu.VMEM((PIXELS, width), dtype) for dtype in (jnp.bfloat16, jnp.float32))
    both = pltpu.VMEM((2, PIXELS, width), jnp.bfloat16)

    def head(chunk, *after):
        send, keep = head_terms(chunk, spots, spread_x, wide, bias, unite, after)
        return keep, lax.ppermute(send, "tp", SWAP)

    far0, far1 = head(0), head(1)
    (far0,) = call_add(far_kernel, "far", [both], *far0)
    across0 = lax.ppermute(far0, "tp", FAR)
    near0 = head(2, far0)
    (far1,) = call_add(far_kernel, "far", [both], *far1)
    across1 = lax.ppermute(far1, "tp", FAR)
    near1 = head(3, far1)
    opposite, following = call_add(near_kernel, "near", [bf16, bf16], *near0, across0)
    opposite, following = lax.ppermute(opposite, "tp", hop(2)), lax.ppermute(following, "tp", hop(1))
    keep1, other1 = near1
    (mid1,) = call_add(mid_kernel, "mid", [pltpu.VMEM((2, PIXELS, width), jnp.float32)], keep1, across1)
    previous, own = call_add(split_kernel, "split", [bf16, f32], mid1, other1)
    previous = lax.ppermute(previous, "tp", hop(3))
    result = added(own, opposite, following, previous).astype(jnp.bfloat16)
    bands = lax.all_to_all(result.reshape(BANDS, LOW, width), "row", 0, 0)
    return bands.reshape(2, 8, LOW, width).transpose(1, 0, 2, 3).reshape(1, 8, 8, width)


def solution(mesh):
    placed = (
        P(None, "row", None, "tp"),
        P(None, "tp", None, None),
        P(None, "tp"),
        P(None, "tp", None),
    )
    return jax.shard_map(
        on_device, mesh=mesh, in_specs=placed, out_specs=P(None, "row", "tp", None), check_vma=False
    )
```

time: 77.1 us -> 70.8 us (0.918); the launches traced: 75.6 us -> 70.4 us
  blocking collectives: 34.4 us -> 12.7 us
  starting transfers between devices: 9.67 us -> 18.9 us
  waiting for transfers between devices: 14.2 us -> 21.8 us
  Pallas kernels: 15.8 us -> 13.4 us
  local copies, waits for them, and re-layouts: 0.86 us -> 3.06 us
    all_to_all x2 -> x1, blocking collectives: 34.4 us -> 12.7 us  [on_device(): bands = lax.all_to_all(result.reshape(BANDS, LOW, width), 'row', 0, 0)]
    ppermute x1 -> x9, starting transfers between devices: 0.09 us -> 9.25 us  [the longest x1 2.99 us: on_device(): across0 = lax.ppermute(far0, 'tp', FAR)]
    ppermute x1 -> x9, waiting for transfers between devices: 2.65 us -> 8.69 us  [the longest x1 5.27 us: on_device(): previous = lax.ppermute(previous, 'tp', hop(3))]
    pallas_call x1, Pallas kernels: 4.15 us -> 1.08 us  [widen(): pl.pallas_call(widen_kernel, out_shape=jax.ShapeDtypeStruct((3, TAPS * ch...]
    unnamed x4 -> x8, local copies, waits for them, and re-layouts: 0.01 us -> 2.27 us
    all_to_all x1, waiting for transfers between devices: 11.5 us -> 13.1 us  [on_device(): mine = lax.all_to_all(packed, 'row', 0, 0)]
    pallas_call x2 -> x11, Pallas kernels: 11.7 us -> 12.4 us  [the longest x4 9.64 us: head_terms(): pl.pallas_call(functools.partial(head_kernel, chunk), in_specs=[pl.BlockS...]
  transfers between devices with their start and end apart: 2 -> 10, of which waited for: 2 -> 5; matrix products, arithmetic and copies ran while one was open for 0% -> 0% of each run, Pallas kernels for 5% -> 12%
where the time goes in v2:
time: 70.8 us; the launch traced here: 70.4 us
  waiting for transfers between devices  21.8 us (31%)
  starting transfers between devices  18.9 us (27%)
  Pallas kernels  13.4 us (19%)
  blocking collectives  12.7 us (18%)
  local copies, waits for them, and re-layouts  3.06 us (4%)
    all_to_all x1, waiting for transfers between devices, on_device(): mine = lax.all_to_all(packed, 'row', 0, 0)  13.1 us
    all_to_all x1, blocking collectives, on_device(): bands = lax.all_to_all(result.reshape(BANDS, LOW, width), 'row', 0, 0)  12.7 us
    pallas_call x4, Pallas kernels, head_terms(): pl.pallas_call(functools.partial(head_kernel, chunk), in_specs=[pl.BlockS...  9.64 us
    all_to_all x1, starting transfers between devices, on_device(): mine = lax.all_to_all(packed, 'row', 0, 0)  9.63 us
    ppermute x1, waiting for transfers between devices, on_device(): previous = lax.ppermute(previous, 'tp', hop(3))  5.27 us
    ppermute x1, starting transfers between devices, on_device(): across0 = lax.ppermute(far0, 'tp', FAR)  2.99 us
    ppermute x1, waiting for transfers between devices, on_device(): across1 = lax.ppermute(far1, 'tp', FAR)  2.35 us
    unnamed x8, local copies, waits for them, and re-layouts  2.27 us
  transfers between devices with their start and end apart: 10, of which 5 were waited for; matrix products, arithmetic and copies ran while one was open for 0% of the time, Pallas kernels for 12%

profile of v2, /device:TPU:6, one launch (start us, length us, event | category | flops | bytes accessed | tf_op | source)
XLA Modules:
  0.0 70.4 jit_solution(16936388272523844916)
XLA Ops:
  0.0 0.0 copy-start.2
  0.0 1.0 %copy-done.2 = bf16[1,8,128,256]{3,2,1,0:T(8,128)(2,1)S(1)} copy-done((bf16[1,8,128,256]{3,2,1,0:T(8,128)(2,1)S(1)}, bf16[1,8,128,256]{3,2,1,0:T(8,128)(2,1)}, u32[]{:S(2)}) %copy-start.2) | copy-done | bytes 524312
  1.0 0.9 %pack.1 = bf16[16,64,256]{2,1,0:T(8,128)(2,1)} custom-call(bf16[8,128,256]{2,1,0:T(8,128)(2,1)S(1)} %bitcast.31), custom_call_target="tpu_custom_call" | custom-call | tf_op jit(solution)/shard_map/pack/pallas_call | solution.py:43
  2.0 9.6 %all-to-all-start = ((bf16[16,64,256]{2,1,0:T(8,128)(2,1)}), bf16[16,64,256]{2,1,0:T(8,128)(2,1)}, u32[]{:S(2)}, u32[]{:S(2)}) async-start(bf16[16,64,256]{2,1,0:T(8,128)(2,1)} %pack.1), calls=%async_computation | async-start | bytes 1048576 | tf_op jit(solution)/shard_map/all_to_all | solution.py:213
  11.8 0.0 copy-start.1
  11.8 1.2 %copy-done.1 = bf16[3,4,64,576]{3,2,1,0:T(8,128)(2,1)S(1)} copy-done((bf16[3,4,64,576]{3,2,1,0:T(8,128)(2,1)S(1)}, bf16[3,4,64,576]{3,2,1,0:T(8,128)(2,1)}, u32[]{:S(2)}) %copy-start.1) | copy-done | bytes 884760
  13.0 1.1 %widen.1.w_ref = bf16[3,2304,256]{2,1,0:T(8,128)(2,1)S(1)} custom-call(bf16[3,256,576]{2,1,0:T(8,128)(2,1)S(1)} %bitcast.30), custom_call_target="tpu_custom_call" | custom-call | tf_op jit(solution)/shard_map/widen/pallas_call | solution.py:70
  14.1 0.0 copy-start.3
  14.1 0.1 add_bitcast_fusion
  14.2 0.1 add_bitcast_fusion.2
  14.2 13.1 %all-to-all-done.x_ref = bf16[16,64,256]{2,1,0:T(8,128)(2,1)} async-done(((bf16[16,64,256]{2,1,0:T(8,128)(2,1)}), bf16[16,64,256]{2,1,0:T(8,128)(2,1)}, u32[]{:S(2)}, u32[]{:S(2)}) %all-to-all-start) | async-done | bytes 524320 | tf_op jit(solution)/shard_map/all_to_all | solution.py:213
  27.4 0.0 copy-start
  27.4 1.5 %spread.1.s_ref = bf16[7,24,64,256]{3,2,1,0:T(8,128)(2,1)S(1)} custom-call(bf16[16,64,256]{2,1,0:T(8,128)(2,1)} %all-to-all-done.x_ref), custom_call_target="tpu_custom_call" | custom-call | tf_op jit(solution)/shard_map/spread/pallas_call | solution.py:113
  28.9 0.0 copy-done.3
  28.9 0.0 copy-done
  28.9 2.4 %head.6 = (bf16[2,64,1024]{2,1,0:T(8,128)(2,1)S(1)}, f32[2,64,1024]{2,1,0:T(8,128)S(1)}) custom-call(s32[4,4]{1,0:T(4,128)S(1)} %pad_add_fusion.spot_ref, bf16[7,24,64,256]{3,2,1,0:T(8,128)(2,1)S(1)} %spread.1.s_ref, bf16[3,2304,256]{2,1,0:T(8,128)(2,1)S(1)} %widen.1.w_ref, f32[3,256]{1,0:T(4,128)S(1)} %copy-done.3, bf16[3,256,1024]{2,1,0:T(8,128)(2,1)S(1)} %copy-done), custom_call_target="tpu_custom_call" | custom-call | tf_op jit(solution)/shard_map/head/pallas_call | solution.py:185
  31.3 0.1 collective-permute-start.3
  31.4 2.4 %head.4 = (bf16[2,64,1024]{2,1,0:T(8,128)(2,1)S(1)}, f32[2,64,1024]{2,1,0:T(8,128)S(1)}) custom-call(s32[4,4]{1,0:T(4,128)S(1)} %pad_add_fusion.spot_ref, bf16[7,24,64,256]{3,2,1,0:T(8,128)(2,1)S(1)} %spread.1.s_ref, bf16[3,2304,256]{2,1,0:T(8,128)(2,1)S(1)} %widen.1.w_ref, f32[3,256]{1,0:T(4,128)S(1)} %copy-done.3, bf16[3,256,1024]{2,1,0:T(8,128)(2,1)S(1)} %copy-done), custom_call_target="tpu_custom_call" | custom-call | tf_op jit(solution)/shard_map/head/pallas_call | solution.py:185
  33.8 0.6 collective-permute-start
  34.4 0.0 collective-permute-done.3.other_ref
  34.4 0.1 far.3.refs_0_
  34.5 3.0 %collective-permute-start.5 = (bf16[2,64,1024]{2,1,0:T(8,128)(2,1)S(1)}, bf16[2,64,1024]{2,1,0:T(8,128)(2,1)S(1)}, u32[]{:S(2)}, u32[]{:S(2)}) collective-permute-start(bf16[2,64,1024]{2,1,0:T(8,128)(2,1)S(1)} %far.3.refs_0_), channel_id=1, source_target_pairs={{0,2},{1,3},{2,0},{3,1},{4,6},{5,7},{6,4},{7,5},{8,10},{9,11},{10,... | collective-permute-start | bytes 786440 | tf_op jit(solution)/shard_map/ppermute | solution.py:226
  37.5 2.4 %head.7 = (bf16[2,64,1024]{2,1,0:T(8,128)(2,1)S(1)}, f32[2,64,1024]{2,1,0:T(8,128)S(1)}) custom-call(s32[4,4]{1,0:T(4,128)S(1)} %pad_add_fusion.spot_ref, bf16[7,24,64,256]{3,2,1,0:T(8,128)(2,1)S(1)} %spread.1.s_ref, bf16[3,2304,256]{2,1,0:T(8,128)(2,1)S(1)} %widen.1.w_ref, f32[3,256]{1,0:T(4,128)S(1)} %copy-done.3, bf16[3,256,1024]{2,1,0:T(8,128)(2,1)S(1)} %copy-done, ...), custom_call_target="tpu_custom_call" | custom-call | tf_op jit(solution)/shard_map/head/pallas_call | solution.py:185
  39.9 0.1 collective-permute-start.4
  40.0 0.0 collective-permute-done.other_ref
  40.1 0.7 %collective-permute-start.1 = (bf16[2,64,1024]{2,1,0:T(8,128)(2,1)S(1)}, bf16[2,64,1024]{2,1,0:T(8,128)(2,1)S(1)}, u32[]{:S(2)}, u32[]{:S(2)}) collective-permute-start(bf16[2,64,1024]{2,1,0:T(8,128)(2,1)S(1)} %far.2.refs_0_), channel_id=1, source_target_pairs={{0,2},{1,3},{2,0},{3,1},{4,6},{5,7},{6,4},{7,5},{8,10},{9,11},{10,... | collective-permute-start | bytes 786440 | tf_op jit(solution)/shard_map/ppermute | solution.py:229
  40.8 2.4 %head.5 = (bf16[2,64,1024]{2,1,0:T(8,128)(2,1)S(1)}, f32[2,64,1024]{2,1,0:T(8,128)S(1)}) custom-call(s32[4,4]{1,0:T(4,128)S(1)} %pad_add_fusion.spot_ref, bf16[7,24,64,256]{3,2,1,0:T(8,128)(2,1)S(1)} %spread.1.s_ref, bf16[3,2304,256]{2,1,0:T(8,128)(2,1)S(1)} %widen.1.w_ref, f32[3,256]{1,0:T(4,128)S(1)} %copy-done.3, bf16[3,256,1024]{2,1,0:T(8,128)(2,1)S(1)} %copy-done, ...), custom_call_target="tpu_custom_call" | custom-call | tf_op jit(solution)/shard_map/head/pallas_call | solution.py:185
  43.2 0.3 collective-permute-start.2
  43.5 0.8 %collective-permute-done.5.across_ref = bf16[2,64,1024]{2,1,0:T(8,128)(2,1)S(1)} collective-permute-done((bf16[2,64,1024]{2,1,0:T(8,128)(2,1)S(1)}, bf16[2,64,1024]{2,1,0:T(8,128)(2,1)S(1)}, u32[]{:S(2)}, u32[]{:S(2)}) %collective-permute-start.5) | collective-permute-done | bytes 262176 | tf_op jit(solution)/shard_map/ppermute | solution.py:226
  44.3 0.0 collective-permute-done.4.other_ref
  44.3 0.1 near.1
  44.4 1.5 %collective-permute-start.6 = (bf16[64,1024]{1,0:T(8,128)(2,1)S(1)}, bf16[64,1024]{1,0:T(8,128)(2,1)S(1)}, u32[]{:S(2)}, u32[]{:S(2)}) collective-permute-start(bf16[64,1024]{1,0:T(8,128)(2,1)S(1)} %get-tuple-element.26), channel_id=1, source_target_pairs={{0,8},{1,9},{2,10},{3,11},{4,12},{5,13},{6,14},{7,15},{8,0},{9,1},... | collective-permute-start | bytes 393224 | tf_op jit(solution)/shard_map/ppermute | solution.py:232
  45.9 2.1 %collective-permute-start.7 = (bf16[64,1024]{1,0:T(8,128)(2,1)S(1)}, bf16[64,1024]{1,0:T(8,128)(2,1)S(1)}, u32[]{:S(2)}, u32[]{:S(2)}) collective-permute-start(bf16[64,1024]{1,0:T(8,128)(2,1)S(1)} %get-tuple-element.27), channel_id=1, source_target_pairs={{0,4},{1,5},{2,6},{3,7},{4,8},{5,9},{6,10},{7,11},{8,12},{9,13},{1... | collective-permute-start | bytes 393224 | tf_op jit(solution)/shard_map/ppermute | solution.py:232
  48.0 2.4 %collective-permute-done.1.across_ref = bf16[2,64,1024]{2,1,0:T(8,128)(2,1)S(1)} collective-permute-done((bf16[2,64,1024]{2,1,0:T(8,128)(2,1)S(1)}, bf16[2,64,1024]{2,1,0:T(8,128)(2,1)S(1)}, u32[]{:S(2)}, u32[]{:S(2)}) %collective-permute-start.1) | collective-permute-done | bytes 262176 | tf_op jit(solution)/shard_map/ppermute | solution.py:229
  50.4 0.0 collective-permute-done.2.other_ref
  50.5 0.9 %collective-permute-start.8 = (bf16[64,1024]{1,0:T(8,128)(2,1)S(1)}, bf16[64,1024]{1,0:T(8,128)(2,1)S(1)}, u32[]{:S(2)}, u32[]{:S(2)}) collective-permute-start(bf16[64,1024]{1,0:T(8,128)(2,1)S(1)} %get-tuple-element.28), channel_id=1, source_target_pairs={{0,12},{1,13},{2,14},{3,15},{4,0},{5,1},{6,2},{7,3},{8,4},{9,5},{1... | collective-permute-start | bytes 393224 | tf_op jit(solution)/shard_map/ppermute | solution.py:236
  51.4 0.0 collective-permute-done.6
  51.4 0.2 collective-permute-done.7
  51.6 5.3 %collective-permute-done.8 = bf16[64,1024]{1,0:T(8,128)(2,1)S(1)} collective-permute-done((bf16[64,1024]{1,0:T(8,128)(2,1)S(1)}, bf16[64,1024]{1,0:T(8,128)(2,1)S(1)}, u32[]{:S(2)}, u32[]{:S(2)}) %collective-permute-start.8) | collective-permute-done | bytes 131104 | tf_op jit(solution)/shard_map/ppermute | solution.py:236
  56.9 0.1 add_convert_fusion
  56.9 0.1 reshape.13
  57.0 12.7 %all_to_all.10 = bf16[16,4,1024]{2,1,0:T(4,128)(2,1)S(1)} all-to-all(bf16[16,4,1024]{2,1,0:T(4,128)(2,1)S(1)} %reshape.13), channel_id=1, replica_groups=mesh['row'=16,'tp'=16] {'row'}, dimensions={0} | all-to-all | bytes 262144 | tf_op jit(solution)/shard_map/all_to_all | solution.py:238
  69.8 0.7 reshape.15
  (5 shorter events, 0.2 us)
Async XLA Ops:
  0.0 1.0 %copy-start.2 = (bf16[1,8,128,256]{3,2,1,0:T(8,128)(2,1)S(1)}, bf16[1,8,128,256]{3,2,1,0:T(8,128)(2,1)}, u32[]{:S(2)}) copy-start(bf16[1,8,128,256]{3,2,1,0:T(8,128)(2,1)} %param.4) | copy-start | bytes 1572868
  2.0 25.4 %all-to-all-start = ((bf16[16,64,256]{2,1,0:T(8,128)(2,1)}), bf16[16,64,256]{2,1,0:T(8,128)(2,1)}, u32[]{:S(2)}, u32[]{:S(2)}) async-start(bf16[16,64,256]{2,1,0:T(8,128)(2,1)} %pack.1), calls=%async_computation | async-start | bytes 1048576 | tf_op jit(solution)/shard_map/all_to_all | solution.py:213
  11.8 1.2 %copy-start.1 = (bf16[3,4,64,576]{3,2,1,0:T(8,128)(2,1)S(1)}, bf16[3,4,64,576]{3,2,1,0:T(8,128)(2,1)}, u32[]{:S(2)}) copy-start(bf16[3,4,64,576]{3,2,1,0:T(8,128)(2,1)} %param.5) | copy-start | bytes 2654212
  14.1 14.8 %copy-start.3 = (f32[3,256]{1,0:T(4,128)S(1)}, f32[3,256]{1,0:T(4,128)}, u32[]{:S(2)}) copy-start(f32[3,256]{1,0:T(4,128)} %bias_ref.7) | copy-start | bytes 9220
  27.4 1.6 %copy-start = (bf16[3,256,1024]{2,1,0:T(8,128)(2,1)S(1)}, bf16[3,256,1024]{2,1,0:T(8,128)(2,1)}, u32[]{:S(2)}) copy-start(bf16[3,256,1024]{2,1,0:T(8,128)(2,1)} %unite_ref.7) | copy-start | bytes 4718596
  31.3 3.1 %collective-permute-start.3 = (bf16[2,64,1024]{2,1,0:T(8,128)(2,1)S(1)}, bf16[2,64,1024]{2,1,0:T(8,128)(2,1)S(1)}, u32[]{:S(2)}, u32[]{:S(2)}) collective-permute-start(bf16[2,64,1024]{2,1,0:T(8,128)(2,1)S(1)} %get-tuple-element.23), channel_id=1, source_target_pairs={{0,1},{1,0},{2,3},{3,2},{4,5},{5,4},{6,7},{7,6},{8,9},{9,8},{10,11... | collective-permute-start | bytes 786440 | tf_op jit(solution)/shard_map/ppermute | solution.py:222
  33.8 6.2 %collective-permute-start = (bf16[2,64,1024]{2,1,0:T(8,128)(2,1)S(1)}, bf16[2,64,1024]{2,1,0:T(8,128)(2,1)S(1)}, u32[]{:S(2)}, u32[]{:S(2)}) collective-permute-start(bf16[2,64,1024]{2,1,0:T(8,128)(2,1)S(1)} %get-tuple-element.18), channel_id=1, source_target_pairs={{0,1},{1,0},{2,3},{3,2},{4,5},{5,4},{6,7},{7,6},{8,9},{9,8},{10,11... | collective-permute-start | bytes 786440 | tf_op jit(solution)/shard_map/ppermute | solution.py:222
  34.5 9.8 %collective-permute-start.5 = (bf16[2,64,1024]{2,1,0:T(8,128)(2,1)S(1)}, bf16[2,64,1024]{2,1,0:T(8,128)(2,1)S(1)}, u32[]{:S(2)}, u32[]{:S(2)}) collective-permute-start(bf16[2,64,1024]{2,1,0:T(8,128)(2,1)S(1)} %far.3.refs_0_), channel_id=1, source_target_pairs={{0,2},{1,3},{2,0},{3,1},{4,6},{5,7},{6,4},{7,5},{8,10},{9,11},{10,... | collective-permute-start | bytes 786440 | tf_op jit(solution)/shard_map/ppermute | solution.py:226
  39.9 4.4 %collective-permute-start.4 = (bf16[2,64,1024]{2,1,0:T(8,128)(2,1)S(1)}, bf16[2,64,1024]{2,1,0:T(8,128)(2,1)S(1)}, u32[]{:S(2)}, u32[]{:S(2)}) collective-permute-start(bf16[2,64,1024]{2,1,0:T(8,128)(2,1)S(1)} %get-tuple-element.25), channel_id=1, source_target_pairs={{0,1},{1,0},{2,3},{3,2},{4,5},{5,4},{6,7},{7,6},{8,9},{9,8},{10,11... | collective-permute-start | bytes 786440 | tf_op jit(solution)/shard_map/ppermute | solution.py:222
  40.1 10.3 %collective-permute-start.1 = (bf16[2,64,1024]{2,1,0:T(8,128)(2,1)S(1)}, bf16[2,64,1024]{2,1,0:T(8,128)(2,1)S(1)}, u32[]{:S(2)}, u32[]{:S(2)}) collective-permute-start(bf16[2,64,1024]{2,1,0:T(8,128)(2,1)S(1)} %far.2.refs_0_), channel_id=1, source_target_pairs={{0,2},{1,3},{2,0},{3,1},{4,6},{5,7},{6,4},{7,5},{8,10},{9,11},{10,... | collective-permute-start | bytes 786440 | tf_op jit(solution)/shard_map/ppermute | solution.py:229
  43.2 7.2 %collective-permute-start.2 = (bf16[2,64,1024]{2,1,0:T(8,128)(2,1)S(1)}, bf16[2,64,1024]{2,1,0:T(8,128)(2,1)S(1)}, u32[]{:S(2)}, u32[]{:S(2)}) collective-permute-start(bf16[2,64,1024]{2,1,0:T(8,128)(2,1)S(1)} %get-tuple-element.20), channel_id=1, source_target_pairs={{0,1},{1,0},{2,3},{3,2},{4,5},{5,4},{6,7},{7,6},{8,9},{9,8},{10,11... | collective-permute-start | bytes 786440 | tf_op jit(solution)/shard_map/ppermute | solution.py:222
  44.4 7.0 %collective-permute-start.6 = (bf16[64,1024]{1,0:T(8,128)(2,1)S(1)}, bf16[64,1024]{1,0:T(8,128)(2,1)S(1)}, u32[]{:S(2)}, u32[]{:S(2)}) collective-permute-start(bf16[64,1024]{1,0:T(8,128)(2,1)S(1)} %get-tuple-element.26), channel_id=1, source_target_pairs={{0,8},{1,9},{2,10},{3,11},{4,12},{5,13},{6,14},{7,15},{8,0},{9,1},... | collective-permute-start | bytes 393224 | tf_op jit(solution)/shard_map/ppermute | solution.py:232
  45.9 5.7 %collective-permute-start.7 = (bf16[64,1024]{1,0:T(8,128)(2,1)S(1)}, bf16[64,1024]{1,0:T(8,128)(2,1)S(1)}, u32[]{:S(2)}, u32[]{:S(2)}) collective-permute-start(bf16[64,1024]{1,0:T(8,128)(2,1)S(1)} %get-tuple-element.27), channel_id=1, source_target_pairs={{0,4},{1,5},{2,6},{3,7},{4,8},{5,9},{6,10},{7,11},{8,12},{9,13},{1... | collective-permute-start | bytes 393224 | tf_op jit(solution)/shard_map/ppermute | solution.py:232
  50.5 6.4 %collective-permute-start.8 = (bf16[64,1024]{1,0:T(8,128)(2,1)S(1)}, bf16[64,1024]{1,0:T(8,128)(2,1)S(1)}, u32[]{:S(2)}, u32[]{:S(2)}) collective-permute-start(bf16[64,1024]{1,0:T(8,128)(2,1)S(1)} %get-tuple-element.28), channel_id=1, source_target_pairs={{0,12},{1,13},{2,14},{3,15},{4,0},{5,1},{6,2},{7,3},{8,4},{9,5},{1... | collective-permute-start | bytes 393224 | tf_op jit(solution)/shard_map/ppermute | solution.py:236

commit v3 on v2

--- a/solution.py
+++ b/solution.py
@@ -15,6 +15,7 @@
 PIXELS = BANDS * LOW
 PAD = 4
 TAPS = 9
+GROUP = 64
 VMEM_SPEC = pl.BlockSpec(memory_space=pltpu.VMEM)
 
 
@@ -49,29 +50,26 @@
     )(x)
 
 
-def widen_kernel(w_ref, out_ref):
-    chan = w_ref.shape[1]
-    rows = lax.broadcasted_iota(jnp.int32, (chan, chan), 0) // 64
-    cols = lax.broadcasted_iota(jnp.int32, (chan, chan), 1) // 64
-    same = rows == cols
+def turn_kernel(w_ref, out_ref):
     for tap in range(TAPS):
         start, width = (tap // 2) * 128, 128 if tap < 8 else 64
-        shift = (tap % 2) * 64
-        place = lax.broadcasted_iota(jnp.int32, (chan, width), 0) % 64 + shift
-        pick = (place == lax.broadcasted_iota(jnp.int32, (chan, width), 1)).astype(jnp.float32).astype(jnp.bfloat16)
+        place = lax.broadcasted_iota(jnp.int32, (GROUP, width), 0) + (tap % 2) * GROUP
+        pick = (place == lax.broadcasted_iota(jnp.int32, (GROUP, width), 1)).astype(jnp.float32).astype(jnp.bfloat16)
         for arm in range(3):
             slab = w_ref[arm, :, start : start + width]
-            wide = lax.dot_general(pick, slab, (((1,), (1,)), ((), ())), preferred_element_type=jnp.float32)
-            out_ref[arm, tap * chan : (tap + 1) * chan, :] = jnp.where(same, wide, 0.0).astype(jnp.bfloat16)
-
-
-def widen(conv_weight):
+            turned = lax.dot_general(pick, slab, (((1,), (1,)), ((), ())), preferred_element_type=jnp.float32)
+            out_ref[arm, tap * GROUP : (tap + 1) * GROUP, :] = turned.astype(jnp.bfloat16)
+
+
+def turn(conv_weight):
     chan = conv_weight.shape[1] * conv_weight.shape[2]
     return pl.pallas_call(
-        widen_kernel,
-        out_shape=jax.ShapeDtypeStruct((3, TAPS * chan, chan), jnp.bfloat16),
-        compiler_params=pltpu.CompilerParams(vmem_limit_bytes=16 * 2**20),
-        name="widen",
+        turn_kernel,
+        in_specs=[VMEM_SPEC],
+        out_specs=VMEM_SPEC,
+        out_shape=pltpu.VMEM((3, TAPS * GROUP, chan), jnp.bfloat16),
+        compiler_params=pltpu.CompilerParams(vmem_limit_bytes=16 * 2**20),
+        name="turn",
     )(conv_weight.reshape(3, chan, -1))
 
 
@@ -159,6 +157,9 @@
     send_ref, keep_ref = refs[-2:]
     chan = s_ref.shape[3]
     spots = [PAD + spot_ref[chunk, at] for at in range(4)]
+    groups = chan // GROUP
+    column = lax.broadcasted_iota(jnp.int32, (GROUP, chan), 1) // GROUP
+    masks = [(column == group).astype(jnp.float32).astype(jnp.bfloat16) for group in range(groups)]
     hidden = []
     for arm, distance in enumerate(DISTANCES):
         total = None
@@ -167,7 +168,9 @@
             for kw in range(3):
                 left = jnp.concatenate([s_ref[at, spot + (kw - 1) * distance] for spot in spots], axis=0)
                 tap = 3 * kh + kw
-                part = jnp.dot(left, w_ref[arm, tap * chan : (tap + 1) * chan, :], preferred_element_type=jnp.float32)
+                narrow = w_ref[arm, tap * GROUP : (tap + 1) * GROUP, :]
+                wide = jnp.concatenate([narrow * mask for mask in masks], axis=0)
+                part = jnp.dot(left, wide, preferred_element_type=jnp.float32)
                 total = part if total is None else total + part
         summed = total + bias_ref[arm : arm + 1, :]
         hidden.append((0.5 * summed * (1.0 + lax.erf(summed * (0.5**0.5)))).astype(jnp.bfloat16))
@@ -209,7 +212,7 @@
         for chunk in CHUNKS
     ])
     packed = pack(feature_map[0])
-    wide = in_vmem(widen(conv_weight))
+    wide = in_vmem(turn(conv_weight))
     mine = lax.all_to_all(packed, "row", 0, 0)
     spread_x = spread(mine)
     unite, bias = in_vmem(unite_weight), in_vmem(branch_bias)

time: 70.8 us -> 69.6 us (0.983)
  Pallas kernels: 13.4 us -> 12 us
    pallas_call x1, Pallas kernels: 1.53 us -> 0.37 us  [spread(): pl.pallas_call(spread_kernel, in_specs=[VMEM_SPEC], out_specs=VMEM_SPEC,...]
where the time goes in v3:
time: 69.6 us; the launch traced here: 69.3 us
  waiting for transfers between devices  22.1 us (32%)
  starting transfers between devices  18.8 us (27%)
  blocking collectives  12.7 us (18%)
  Pallas kernels  12 us (17%)
  local copies, waits for them, and re-layouts  3.16 us (5%)
    all_to_all x1, waiting for transfers between devices, on_device(): mine = lax.all_to_all(packed, 'row', 0, 0)  13.4 us
    all_to_all x1, blocking collectives, on_device(): bands = lax.all_to_all(result.reshape(BANDS, LOW, width), 'row', 0, 0)  12.7 us
    pallas_call x4, Pallas kernels, head_terms(): pl.pallas_call(functools.partial(head_kernel, chunk), in_specs=[pl.BlockS...  9.73 us
    all_to_all x1, starting transfers between devices, on_device(): mine = lax.all_to_all(packed, 'row', 0, 0)  9.58 us
    ppermute x1, waiting for transfers between devices, on_device(): previous = lax.ppermute(previous, 'tp', hop(3))  5.29 us
    ppermute x1, starting transfers between devices, on_device(): across0 = lax.ppermute(far0, 'tp', FAR)  2.99 us
    ppermute x1, waiting for transfers between devices, on_device(): across1 = lax.ppermute(far1, 'tp', FAR)  2.37 us
    unnamed x8, local copies, waits for them, and re-layouts  2.36 us
  transfers between devices with their start and end apart: 10, of which 5 were waited for; matrix products, arithmetic and copies ran while one was open for 0% of the time, Pallas kernels for 12%

profile of v3, /device:TPU:6, one launch (start us, length us, event | category | flops | bytes accessed | tf_op | source)
XLA Modules:
  0.0 69.3 jit_solution(12624011344452388526)
XLA Ops:
  0.0 0.0 copy-start
  0.0 0.0 copy-start.2
  0.0 1.2 %copy-done.2 = bf16[1,8,128,256]{3,2,1,0:T(8,128)(2,1)S(1)} copy-done((bf16[1,8,128,256]{3,2,1,0:T(8,128)(2,1)S(1)}, bf16[1,8,128,256]{3,2,1,0:T(8,128)(2,1)}, u32[]{:S(2)}) %copy-start.2) | copy-done | bytes 524312
  1.2 0.0 copy-start.3
  1.2 0.9 %pack.1 = bf16[16,64,256]{2,1,0:T(8,128)(2,1)} custom-call(bf16[8,128,256]{2,1,0:T(8,128)(2,1)S(1)} %bitcast.31), custom_call_target="tpu_custom_call" | custom-call | tf_op jit(solution)/shard_map/pack/pallas_call | solution.py:44
  2.1 9.6 %all-to-all-start = ((bf16[16,64,256]{2,1,0:T(8,128)(2,1)}), bf16[16,64,256]{2,1,0:T(8,128)(2,1)S(1)}, u32[]{:S(2)}, u32[]{:S(2)}) async-start(bf16[16,64,256]{2,1,0:T(8,128)(2,1)} %pack.1), calls=%async_computation | async-start | bytes 1048576 | tf_op jit(solution)/shard_map/all_to_all | solution.py:216
  11.8 0.0 copy-start.1
  11.9 1.2 %copy-done.1 = bf16[3,4,64,576]{3,2,1,0:T(8,128)(2,1)S(1)} copy-done((bf16[3,4,64,576]{3,2,1,0:T(8,128)(2,1)S(1)}, bf16[3,4,64,576]{3,2,1,0:T(8,128)(2,1)}, u32[]{:S(2)}) %copy-start.1) | copy-done | bytes 884760
  13.0 0.7 %turn.1.w_ref = bf16[3,576,256]{2,1,0:T(8,128)(2,1)S(1)} custom-call(bf16[3,256,576]{2,1,0:T(8,128)(2,1)S(1)} %bitcast.30), custom_call_target="tpu_custom_call" | custom-call | tf_op jit(solution)/shard_map/turn/pallas_call | solution.py:66
  13.8 0.1 add_bitcast_fusion
  13.9 0.1 add_bitcast_fusion.2
  14.0 13.4 %all-to-all-done.x_ref = bf16[16,64,256]{2,1,0:T(8,128)(2,1)S(1)} async-done(((bf16[16,64,256]{2,1,0:T(8,128)(2,1)}), bf16[16,64,256]{2,1,0:T(8,128)(2,1)S(1)}, u32[]{:S(2)}, u32[]{:S(2)}) %all-to-all-start) | async-done | bytes 524320 | tf_op jit(solution)/shard_map/all_to_all | solution.py:216
  27.4 0.4 spread.1.s_ref
  27.8 0.0 copy-done
  27.8 0.0 copy-done.3
  27.8 2.4 %head.6 = (bf16[2,64,1024]{2,1,0:T(8,128)(2,1)S(1)}, f32[2,64,1024]{2,1,0:T(8,128)S(1)}) custom-call(s32[4,4]{1,0:T(4,128)S(1)} %pad_add_fusion.spot_ref, bf16[7,24,64,256]{3,2,1,0:T(8,128)(2,1)S(1)} %spread.1.s_ref, bf16[3,576,256]{2,1,0:T(8,128)(2,1)S(1)} %turn.1.w_ref, f32[3,256]{1,0:T(4,128)S(1)} %copy-done.3, bf16[3,256,1024]{2,1,0:T(8,128)(2,1)S(1)} %copy-done), custom_call_target="tpu_custom_call" | custom-call | tf_op jit(solution)/shard_map/head/pallas_call | solution.py:188
  30.2 0.1 collective-permute-start.3
  30.3 2.4 %head.4 = (bf16[2,64,1024]{2,1,0:T(8,128)(2,1)S(1)}, f32[2,64,1024]{2,1,0:T(8,128)S(1)}) custom-call(s32[4,4]{1,0:T(4,128)S(1)} %pad_add_fusion.spot_ref, bf16[7,24,64,256]{3,2,1,0:T(8,128)(2,1)S(1)} %spread.1.s_ref, bf16[3,576,256]{2,1,0:T(8,128)(2,1)S(1)} %turn.1.w_ref, f32[3,256]{1,0:T(4,128)S(1)} %copy-done.3, bf16[3,256,1024]{2,1,0:T(8,128)(2,1)S(1)} %copy-done), custom_call_target="tpu_custom_call" | custom-call | tf_op jit(solution)/shard_map/head/pallas_call | solution.py:188
  32.8 0.6 collective-permute-start
  33.3 0.0 collective-permute-done.3.other_ref
  33.4 3.0 %collective-permute-start.5 = (bf16[2,64,1024]{2,1,0:T(8,128)(2,1)S(1)}, bf16[2,64,1024]{2,1,0:T(8,128)(2,1)S(1)}, u32[]{:S(2)}, u32[]{:S(2)}) collective-permute-start(bf16[2,64,1024]{2,1,0:T(8,128)(2,1)S(1)} %far.3.refs_0_), channel_id=1, source_target_pairs={{0,2},{1,3},{2,0},{3,1},{4,6},{5,7},{6,4},{7,5},{8,10},{9,11},{10,... | collective-permute-start | bytes 786440 | tf_op jit(solution)/shard_map/ppermute | solution.py:229
  36.4 2.4 %head.7 = (bf16[2,64,1024]{2,1,0:T(8,128)(2,1)S(1)}, f32[2,64,1024]{2,1,0:T(8,128)S(1)}) custom-call(s32[4,4]{1,0:T(4,128)S(1)} %pad_add_fusion.spot_ref, bf16[7,24,64,256]{3,2,1,0:T(8,128)(2,1)S(1)} %spread.1.s_ref, bf16[3,576,256]{2,1,0:T(8,128)(2,1)S(1)} %turn.1.w_ref, f32[3,256]{1,0:T(4,128)S(1)} %copy-done.3, bf16[3,256,1024]{2,1,0:T(8,128)(2,1)S(1)} %copy-done, ...), custom_call_target="tpu_custom_call" | custom-call | tf_op jit(solution)/shard_map/head/pallas_call | solution.py:188
  38.8 0.1 collective-permute-start.4
  38.9 0.0 collective-permute-done.other_ref
  39.0 0.7 %collective-permute-start.1 = (bf16[2,64,1024]{2,1,0:T(8,128)(2,1)S(1)}, bf16[2,64,1024]{2,1,0:T(8,128)(2,1)S(1)}, u32[]{:S(2)}, u32[]{:S(2)}) collective-permute-start(bf16[2,64,1024]{2,1,0:T(8,128)(2,1)S(1)} %far.2.refs_0_), channel_id=1, source_target_pairs={{0,2},{1,3},{2,0},{3,1},{4,6},{5,7},{6,4},{7,5},{8,10},{9,11},{10,... | collective-permute-start | bytes 786440 | tf_op jit(solution)/shard_map/ppermute | solution.py:232
  39.7 2.4 %head.5 = (bf16[2,64,1024]{2,1,0:T(8,128)(2,1)S(1)}, f32[2,64,1024]{2,1,0:T(8,128)S(1)}) custom-call(s32[4,4]{1,0:T(4,128)S(1)} %pad_add_fusion.spot_ref, bf16[7,24,64,256]{3,2,1,0:T(8,128)(2,1)S(1)} %spread.1.s_ref, bf16[3,576,256]{2,1,0:T(8,128)(2,1)S(1)} %turn.1.w_ref, f32[3,256]{1,0:T(4,128)S(1)} %copy-done.3, bf16[3,256,1024]{2,1,0:T(8,128)(2,1)S(1)} %copy-done, ...), custom_call_target="tpu_custom_call" | custom-call | tf_op jit(solution)/shard_map/head/pallas_call | solution.py:188
  42.1 0.3 collective-permute-start.2
  42.4 0.8 %collective-permute-done.5.across_ref = bf16[2,64,1024]{2,1,0:T(8,128)(2,1)S(1)} collective-permute-done((bf16[2,64,1024]{2,1,0:T(8,128)(2,1)S(1)}, bf16[2,64,1024]{2,1,0:T(8,128)(2,1)S(1)}, u32[]{:S(2)}, u32[]{:S(2)}) %collective-permute-start.5) | collective-permute-done | bytes 262176 | tf_op jit(solution)/shard_map/ppermute | solution.py:229
  43.2 0.0 collective-permute-done.4.other_ref
  43.2 0.1 near.1
  43.3 1.5 %collective-permute-start.6 = (bf16[64,1024]{1,0:T(8,128)(2,1)S(1)}, bf16[64,1024]{1,0:T(8,128)(2,1)S(1)}, u32[]{:S(2)}, u32[]{:S(2)}) collective-permute-start(bf16[64,1024]{1,0:T(8,128)(2,1)S(1)} %get-tuple-element.26), channel_id=1, source_target_pairs={{0,8},{1,9},{2,10},{3,11},{4,12},{5,13},{6,14},{7,15},{8,0},{9,1},... | collective-permute-start | bytes 393224 | tf_op jit(solution)/shard_map/ppermute | solution.py:235
  44.8 2.1 %collective-permute-start.7 = (bf16[64,1024]{1,0:T(8,128)(2,1)S(1)}, bf16[64,1024]{1,0:T(8,128)(2,1)S(1)}, u32[]{:S(2)}, u32[]{:S(2)}) collective-permute-start(bf16[64,1024]{1,0:T(8,128)(2,1)S(1)} %get-tuple-element.27), channel_id=1, source_target_pairs={{0,4},{1,5},{2,6},{3,7},{4,8},{5,9},{6,10},{7,11},{8,12},{9,13},{1... | collective-permute-start | bytes 393224 | tf_op jit(solution)/shard_map/ppermute | solution.py:235
  46.9 2.4 %collective-permute-done.1.across_ref = bf16[2,64,1024]{2,1,0:T(8,128)(2,1)S(1)} collective-permute-done((bf16[2,64,1024]{2,1,0:T(8,128)(2,1)S(1)}, bf16[2,64,1024]{2,1,0:T(8,128)(2,1)S(1)}, u32[]{:S(2)}, u32[]{:S(2)}) %collective-permute-start.1) | collective-permute-done | bytes 262176 | tf_op jit(solution)/shard_map/ppermute | solution.py:232
  49.3 0.0 collective-permute-done.2.other_ref
  49.4 0.9 %collective-permute-start.8 = (bf16[64,1024]{1,0:T(8,128)(2,1)S(1)}, bf16[64,1024]{1,0:T(8,128)(2,1)S(1)}, u32[]{:S(2)}, u32[]{:S(2)}) collective-permute-start(bf16[64,1024]{1,0:T(8,128)(2,1)S(1)} %get-tuple-element.28), channel_id=1, source_target_pairs={{0,12},{1,13},{2,14},{3,15},{4,0},{5,1},{6,2},{7,3},{8,4},{9,5},{1... | collective-permute-start | bytes 393224 | tf_op jit(solution)/shard_map/ppermute | solution.py:239
  50.3 0.0 collective-permute-done.6
  50.3 0.2 collective-permute-done.7
  50.5 5.3 %collective-permute-done.8 = bf16[64,1024]{1,0:T(8,128)(2,1)S(1)} collective-permute-done((bf16[64,1024]{1,0:T(8,128)(2,1)S(1)}, bf16[64,1024]{1,0:T(8,128)(2,1)S(1)}, u32[]{:S(2)}, u32[]{:S(2)}) %collective-permute-start.8) | collective-permute-done | bytes 131104 | tf_op jit(solution)/shard_map/ppermute | solution.py:239
  55.8 0.1 add_convert_fusion
  55.8 0.1 reshape.13
  55.9 12.7 %all_to_all.10 = bf16[16,4,1024]{2,1,0:T(4,128)(2,1)S(1)} all-to-all(bf16[16,4,1024]{2,1,0:T(4,128)(2,1)S(1)} %reshape.13), channel_id=1, replica_groups=mesh['row'=16,'tp'=16] {'row'}, dimensions={0} | all-to-all | bytes 262144 | tf_op jit(solution)/shard_map/all_to_all | solution.py:241
  68.6 0.7 reshape.15
  (6 shorter events, 0.2 us)
Async XLA Ops:
  0.0 27.8 %copy-start = (bf16[3,256,1024]{2,1,0:T(8,128)(2,1)S(1)}, bf16[3,256,1024]{2,1,0:T(8,128)(2,1)}, u32[]{:S(2)}) copy-start(bf16[3,256,1024]{2,1,0:T(8,128)(2,1)} %unite_ref.7) | copy-start | bytes 4718596
  0.0 1.2 %copy-start.2 = (bf16[1,8,128,256]{3,2,1,0:T(8,128)(2,1)S(1)}, bf16[1,8,128,256]{3,2,1,0:T(8,128)(2,1)}, u32[]{:S(2)}) copy-start(bf16[1,8,128,256]{3,2,1,0:T(8,128)(2,1)} %param.4) | copy-start | bytes 1572868
  1.2 26.6 %copy-start.3 = (f32[3,256]{1,0:T(4,128)S(1)}, f32[3,256]{1,0:T(4,128)}, u32[]{:S(2)}) copy-start(f32[3,256]{1,0:T(4,128)} %bias_ref.7) | copy-start | bytes 9220
  2.1 25.3 %all-to-all-start = ((bf16[16,64,256]{2,1,0:T(8,128)(2,1)}), bf16[16,64,256]{2,1,0:T(8,128)(2,1)S(1)}, u32[]{:S(2)}, u32[]{:S(2)}) async-start(bf16[16,64,256]{2,1,0:T(8,128)(2,1)} %pack.1), calls=%async_computation | async-start | bytes 1048576 | tf_op jit(solution)/shard_map/all_to_all | solution.py:216
  11.8 1.2 %copy-start.1 = (bf16[3,4,64,576]{3,2,1,0:T(8,128)(2,1)S(1)}, bf16[3,4,64,576]{3,2,1,0:T(8,128)(2,1)}, u32[]{:S(2)}) copy-start(bf16[3,4,64,576]{3,2,1,0:T(8,128)(2,1)} %param.5) | copy-start | bytes 2654212
  30.2 3.1 %collective-permute-start.3 = (bf16[2,64,1024]{2,1,0:T(8,128)(2,1)S(1)}, bf16[2,64,1024]{2,1,0:T(8,128)(2,1)S(1)}, u32[]{:S(2)}, u32[]{:S(2)}) collective-permute-start(bf16[2,64,1024]{2,1,0:T(8,128)(2,1)S(1)} %get-tuple-element.23), channel_id=1, source_target_pairs={{0,1},{1,0},{2,3},{3,2},{4,5},{5,4},{6,7},{7,6},{8,9},{9,8},{10,11... | collective-permute-start | bytes 786440 | tf_op jit(solution)/shard_map/ppermute | solution.py:225
  32.8 6.2 %collective-permute-start = (bf16[2,64,1024]{2,1,0:T(8,128)(2,1)S(1)}, bf16[2,64,1024]{2,1,0:T(8,128)(2,1)S(1)}, u32[]{:S(2)}, u32[]{:S(2)}) collective-permute-start(bf16[2,64,1024]{2,1,0:T(8,128)(2,1)S(1)} %get-tuple-element.18), channel_id=1, source_target_pairs={{0,1},{1,0},{2,3},{3,2},{4,5},{5,4},{6,7},{7,6},{8,9},{9,8},{10,11... | collective-permute-start | bytes 786440 | tf_op jit(solution)/shard_map/ppermute | solution.py:225
  33.4 9.8 %collective-permute-start.5 = (bf16[2,64,1024]{2,1,0:T(8,128)(2,1)S(1)}, bf16[2,64,1024]{2,1,0:T(8,128)(2,1)S(1)}, u32[]{:S(2)}, u32[]{:S(2)}) collective-permute-start(bf16[2,64,1024]{2,1,0:T(8,128)(2,1)S(1)} %far.3.refs_0_), channel_id=1, source_target_pairs={{0,2},{1,3},{2,0},{3,1},{4,6},{5,7},{6,4},{7,5},{8,10},{9,11},{10,... | collective-permute-start | bytes 786440 | tf_op jit(solution)/shard_map/ppermute | solution.py:229
  38.8 4.4 %collective-permute-start.4 = (bf16[2,64,1024]{2,1,0:T(8,128)(2,1)S(1)}, bf16[2,64,1024]{2,1,0:T(8,128)(2,1)S(1)}, u32[]{:S(2)}, u32[]{:S(2)}) collective-permute-start(bf16[2,64,1024]{2,1,0:T(8,128)(2,1)S(1)} %get-tuple-element.25), channel_id=1, source_target_pairs={{0,1},{1,0},{2,3},{3,2},{4,5},{5,4},{6,7},{7,6},{8,9},{9,8},{10,11... | collective-permute-start | bytes 786440 | tf_op jit(solution)/shard_map/ppermute | solution.py:225
  39.0 10.3 %collective-permute-start.1 = (bf16[2,64,1024]{2,1,0:T(8,128)(2,1)S(1)}, bf16[2,64,1024]{2,1,0:T(8,128)(2,1)S(1)}, u32[]{:S(2)}, u32[]{:S(2)}) collective-permute-start(bf16[2,64,1024]{2,1,0:T(8,128)(2,1)S(1)} %far.2.refs_0_), channel_id=1, source_target_pairs={{0,2},{1,3},{2,0},{3,1},{4,6},{5,7},{6,4},{7,5},{8,10},{9,11},{10,... | collective-permute-start | bytes 786440 | tf_op jit(solution)/shard_map/ppermute | solution.py:232
  42.1 7.2 %collective-permute-start.2 = (bf16[2,64,1024]{2,1,0:T(8,128)(2,1)S(1)}, bf16[2,64,1024]{2,1,0:T(8,128)(2,1)S(1)}, u32[]{:S(2)}, u32[]{:S(2)}) collective-permute-start(bf16[2,64,1024]{2,1,0:T(8,128)(2,1)S(1)} %get-tuple-element.20), channel_id=1, source_target_pairs={{0,1},{1,0},{2,3},{3,2},{4,5},{5,4},{6,7},{7,6},{8,9},{9,8},{10,11... | collective-permute-start | bytes 786440 | tf_op jit(solution)/shard_map/ppermute | solution.py:225
  43.3 7.0 %collective-permute-start.6 = (bf16[64,1024]{1,0:T(8,128)(2,1)S(1)}, bf16[64,1024]{1,0:T(8,128)(2,1)S(1)}, u32[]{:S(2)}, u32[]{:S(2)}) collective-permute-start(bf16[64,1024]{1,0:T(8,128)(2,1)S(1)} %get-tuple-element.26), channel_id=1, source_target_pairs={{0,8},{1,9},{2,10},{3,11},{4,12},{5,13},{6,14},{7,15},{8,0},{9,1},... | collective-permute-start | bytes 393224 | tf_op jit(solution)/shard_map/ppermute | solution.py:235
  44.8 5.7 %collective-permute-start.7 = (bf16[64,1024]{1,0:T(8,128)(2,1)S(1)}, bf16[64,1024]{1,0:T(8,128)(2,1)S(1)}, u32[]{:S(2)}, u32[]{:S(2)}) collective-permute-start(bf16[64,1024]{1,0:T(8,128)(2,1)S(1)} %get-tuple-element.27), channel_id=1, source_target_pairs={{0,4},{1,5},{2,6},{3,7},{4,8},{5,9},{6,10},{7,11},{8,12},{9,13},{1... | collective-permute-start | bytes 393224 | tf_op jit(solution)/shard_map/ppermute | solution.py:235
  49.4 6.4 %collective-permute-start.8 = (bf16[64,1024]{1,0:T(8,128)(2,1)S(1)}, bf16[64,1024]{1,0:T(8,128)(2,1)S(1)}, u32[]{:S(2)}, u32[]{:S(2)}) collective-permute-start(bf16[64,1024]{1,0:T(8,128)(2,1)S(1)} %get-tuple-element.28), channel_id=1, source_target_pairs={{0,12},{1,13},{2,14},{3,15},{4,0},{5,1},{6,2},{7,3},{8,4},{9,5},{1... | collective-permute-start | bytes 393224 | tf_op jit(solution)/shard_map/ppermute | solution.py:239

commit v4 on v3

--- a/solution.py
+++ b/solution.py
@@ -195,7 +195,7 @@
     )(spots, spread_x, wide, bias, unite, *after)
 
 
-CHUNKS = (((2, 1), (1, 1)), ((3, 1), (0, 1)), ((2, 0), (1, 0)), ((3, 0), (0, 0)))
+CHUNKS = (((2, 1), (3, 1)), ((1, 1), (0, 1)), ((2, 0), (3, 0)), ((1, 0), (0, 0)))
 SWAP = [(i, i ^ 1) for i in range(16)]
 FAR = [(i, i ^ 2) for i in range(16)]
 
@@ -232,11 +232,11 @@
     across1 = lax.ppermute(far1, "tp", FAR)
     near1 = head(3, far1)
     opposite, following = call_add(near_kernel, "near", [bf16, bf16], *near0, across0)
-    opposite, following = lax.ppermute(opposite, "tp", hop(2)), lax.ppermute(following, "tp", hop(1))
+    opposite, following = lax.ppermute(opposite, "tp", hop(2)), lax.ppermute(following, "tp", hop(3))
     keep1, other1 = near1
     (mid1,) = call_add(mid_kernel, "mid", [pltpu.VMEM((2, PIXELS, width), jnp.float32)], keep1, across1)
     previous, own = call_add(split_kernel, "split", [bf16, f32], mid1, other1)
-    previous = lax.ppermute(previous, "tp", hop(3))
+    previous = lax.ppermute(previous, "tp", hop(1))
     result = added(own, opposite, following, previous).astype(jnp.bfloat16)
     bands = lax.all_to_all(result.reshape(BANDS, LOW, width), "row", 0, 0)
     return bands.reshape(2, 8, LOW, width).transpose(1, 0, 2, 3).reshape(1, 8, 8, width)

time: 69.6 us -> 69.1 us (level); the launches traced: 69.3 us -> 68.1 us
  starting transfers between devices: 18.8 us -> 16.4 us
  waiting for transfers between devices: 22.1 us -> 23.3 us
    ppermute x2, starting transfers between devices: 2.99 us -> 0.55 us  [the longest x1 0.55 us: on_device(): previous = lax.ppermute(previous, 'tp', hop(1))]
    ppermute x2, waiting for transfers between devices: 5.49 us -> 3.32 us  [the longest x1 1.93 us: on_device(): previous = lax.ppermute(previous, 'tp', hop(1))]
    ppermute x1, waiting for transfers between devices: 2.37 us -> 4.46 us  [on_device(): across1 = lax.ppermute(far1, 'tp', FAR)]
    ppermute x1, waiting for transfers between devices: 0.01 us -> 1.31 us  [on_device(): lax.ppermute(opposite, 'tp', hop(2))]
  transfers between devices with their start and end apart: 10 -> 10, of which waited for: 5 -> 6; matrix products, arithmetic and copies ran while one was open for 0% -> 0% of each run, Pallas kernels for 12% -> 12%
where the time goes in v4:
time: 69.1 us; the launch traced here: 68.1 us
  waiting for transfers between devices  23.3 us (34%)
  starting transfers between devices  16.4 us (24%)
  blocking collectives  12.7 us (18%)
  Pallas kernels  12 us (17%)
  local copies, waits for them, and re-layouts  3.16 us (5%)
    all_to_all x1, waiting for transfers between devices, on_device(): mine = lax.all_to_all(packed, 'row', 0, 0)  13.4 us
    all_to_all x1, blocking collectives, on_device(): bands = lax.all_to_all(result.reshape(BANDS, LOW, width), 'row', 0, 0)  12.7 us
    pallas_call x4, Pallas kernels, head_terms(): pl.pallas_call(functools.partial(head_kernel, chunk), in_specs=[pl.BlockS...  9.73 us
    all_to_all x1, starting transfers between devices, on_device(): mine = lax.all_to_all(packed, 'row', 0, 0)  9.58 us
    ppermute x1, waiting for transfers between devices, on_device(): across1 = lax.ppermute(far1, 'tp', FAR)  4.46 us
    ppermute x1, starting transfers between devices, on_device(): across0 = lax.ppermute(far0, 'tp', FAR)  2.99 us
    unnamed x8, local copies, waits for them, and re-layouts  2.36 us
    ppermute x1, waiting for transfers between devices, on_device(): previous = lax.ppermute(previous, 'tp', hop(1))  1.93 us
  transfers between devices with their start and end apart: 10, of which 6 were waited for; matrix products, arithmetic and copies ran while one was open for 0% of the time, Pallas kernels for 12%

profile of v4, /device:TPU:6, one launch (start us, length us, event | category | flops | bytes accessed | tf_op | source)
XLA Modules:
  0.0 68.1 jit_solution(8068364678074542560)
XLA Ops:
  0.0 0.0 copy-start
  0.0 0.0 copy-start.2
  0.0 1.2 %copy-done.2 = bf16[1,8,128,256]{3,2,1,0:T(8,128)(2,1)S(1)} copy-done((bf16[1,8,128,256]{3,2,1,0:T(8,128)(2,1)S(1)}, bf16[1,8,128,256]{3,2,1,0:T(8,128)(2,1)}, u32[]{:S(2)}) %copy-start.2) | copy-done | bytes 524312
  1.2 0.0 copy-start.3
  1.2 0.9 %pack.1 = bf16[16,64,256]{2,1,0:T(8,128)(2,1)} custom-call(bf16[8,128,256]{2,1,0:T(8,128)(2,1)S(1)} %bitcast.31), custom_call_target="tpu_custom_call" | custom-call | tf_op jit(solution)/shard_map/pack/pallas_call | solution.py:44
  2.1 9.6 %all-to-all-start = ((bf16[16,64,256]{2,1,0:T(8,128)(2,1)}), bf16[16,64,256]{2,1,0:T(8,128)(2,1)S(1)}, u32[]{:S(2)}, u32[]{:S(2)}) async-start(bf16[16,64,256]{2,1,0:T(8,128)(2,1)} %pack.1), calls=%async_computation | async-start | bytes 1048576 | tf_op jit(solution)/shard_map/all_to_all | solution.py:216
  11.8 0.0 copy-start.1
  11.9 1.2 %copy-done.1 = bf16[3,4,64,576]{3,2,1,0:T(8,128)(2,1)S(1)} copy-done((bf16[3,4,64,576]{3,2,1,0:T(8,128)(2,1)S(1)}, bf16[3,4,64,576]{3,2,1,0:T(8,128)(2,1)}, u32[]{:S(2)}) %copy-start.1) | copy-done | bytes 884760
  13.0 0.7 %turn.1.w_ref = bf16[3,576,256]{2,1,0:T(8,128)(2,1)S(1)} custom-call(bf16[3,256,576]{2,1,0:T(8,128)(2,1)S(1)} %bitcast.30), custom_call_target="tpu_custom_call" | custom-call | tf_op jit(solution)/shard_map/turn/pallas_call | solution.py:66
  13.8 0.1 add_bitcast_fusion
  13.9 0.1 add_bitcast_fusion.2
  14.0 13.4 %all-to-all-done.x_ref = bf16[16,64,256]{2,1,0:T(8,128)(2,1)S(1)} async-done(((bf16[16,64,256]{2,1,0:T(8,128)(2,1)}), bf16[16,64,256]{2,1,0:T(8,128)(2,1)S(1)}, u32[]{:S(2)}, u32[]{:S(2)}) %all-to-all-start) | async-done | bytes 524320 | tf_op jit(solution)/shard_map/all_to_all | solution.py:216
  27.4 0.4 spread.1.s_ref
  27.8 0.0 copy-done
  27.8 0.0 copy-done.3
  27.8 2.4 %head.6 = (bf16[2,64,1024]{2,1,0:T(8,128)(2,1)S(1)}, f32[2,64,1024]{2,1,0:T(8,128)S(1)}) custom-call(s32[4,4]{1,0:T(4,128)S(1)} %pad_add_fusion.spot_ref, bf16[7,24,64,256]{3,2,1,0:T(8,128)(2,1)S(1)} %spread.1.s_ref, bf16[3,576,256]{2,1,0:T(8,128)(2,1)S(1)} %turn.1.w_ref, f32[3,256]{1,0:T(4,128)S(1)} %copy-done.3, bf16[3,256,1024]{2,1,0:T(8,128)(2,1)S(1)} %copy-done), custom_call_target="tpu_custom_call" | custom-call | tf_op jit(solution)/shard_map/head/pallas_call | solution.py:188
  30.2 0.1 collective-permute-start.3
  30.3 2.4 %head.4 = (bf16[2,64,1024]{2,1,0:T(8,128)(2,1)S(1)}, f32[2,64,1024]{2,1,0:T(8,128)S(1)}) custom-call(s32[4,4]{1,0:T(4,128)S(1)} %pad_add_fusion.spot_ref, bf16[7,24,64,256]{3,2,1,0:T(8,128)(2,1)S(1)} %spread.1.s_ref, bf16[3,576,256]{2,1,0:T(8,128)(2,1)S(1)} %turn.1.w_ref, f32[3,256]{1,0:T(4,128)S(1)} %copy-done.3, bf16[3,256,1024]{2,1,0:T(8,128)(2,1)S(1)} %copy-done), custom_call_target="tpu_custom_call" | custom-call | tf_op jit(solution)/shard_map/head/pallas_call | solution.py:188
  32.8 0.6 collective-permute-start
  33.3 0.0 collective-permute-done.3.other_ref
  33.4 3.0 %collective-permute-start.5 = (bf16[2,64,1024]{2,1,0:T(8,128)(2,1)S(1)}, bf16[2,64,1024]{2,1,0:T(8,128)(2,1)S(1)}, u32[]{:S(2)}, u32[]{:S(2)}) collective-permute-start(bf16[2,64,1024]{2,1,0:T(8,128)(2,1)S(1)} %far.3.refs_0_), channel_id=1, source_target_pairs={{0,2},{1,3},{2,0},{3,1},{4,6},{5,7},{6,4},{7,5},{8,10},{9,11},{10,... | collective-permute-start | bytes 786440 | tf_op jit(solution)/shard_map/ppermute | solution.py:229
  36.4 2.4 %head.7 = (bf16[2,64,1024]{2,1,0:T(8,128)(2,1)S(1)}, f32[2,64,1024]{2,1,0:T(8,128)S(1)}) custom-call(s32[4,4]{1,0:T(4,128)S(1)} %pad_add_fusion.spot_ref, bf16[7,24,64,256]{3,2,1,0:T(8,128)(2,1)S(1)} %spread.1.s_ref, bf16[3,576,256]{2,1,0:T(8,128)(2,1)S(1)} %turn.1.w_ref, f32[3,256]{1,0:T(4,128)S(1)} %copy-done.3, bf16[3,256,1024]{2,1,0:T(8,128)(2,1)S(1)} %copy-done, ...), custom_call_target="tpu_custom_call" | custom-call | tf_op jit(solution)/shard_map/head/pallas_call | solution.py:188
  38.8 0.1 collective-permute-start.4
  38.9 0.0 collective-permute-done.other_ref
  39.0 0.7 %collective-permute-start.1 = (bf16[2,64,1024]{2,1,0:T(8,128)(2,1)S(1)}, bf16[2,64,1024]{2,1,0:T(8,128)(2,1)S(1)}, u32[]{:S(2)}, u32[]{:S(2)}) collective-permute-start(bf16[2,64,1024]{2,1,0:T(8,128)(2,1)S(1)} %far.2.refs_0_), channel_id=1, source_target_pairs={{0,2},{1,3},{2,0},{3,1},{4,6},{5,7},{6,4},{7,5},{8,10},{9,11},{10,... | collective-permute-start | bytes 786440 | tf_op jit(solution)/shard_map/ppermute | solution.py:232
  39.7 2.4 %head.5 = (bf16[2,64,1024]{2,1,0:T(8,128)(2,1)S(1)}, f32[2,64,1024]{2,1,0:T(8,128)S(1)}) custom-call(s32[4,4]{1,0:T(4,128)S(1)} %pad_add_fusion.spot_ref, bf16[7,24,64,256]{3,2,1,0:T(8,128)(2,1)S(1)} %spread.1.s_ref, bf16[3,576,256]{2,1,0:T(8,128)(2,1)S(1)} %turn.1.w_ref, f32[3,256]{1,0:T(4,128)S(1)} %copy-done.3, bf16[3,256,1024]{2,1,0:T(8,128)(2,1)S(1)} %copy-done, ...), custom_call_target="tpu_custom_call" | custom-call | tf_op jit(solution)/shard_map/head/pallas_call | solution.py:188
  42.1 0.3 collective-permute-start.2
  42.4 0.8 %collective-permute-done.5.across_ref = bf16[2,64,1024]{2,1,0:T(8,128)(2,1)S(1)} collective-permute-done((bf16[2,64,1024]{2,1,0:T(8,128)(2,1)S(1)}, bf16[2,64,1024]{2,1,0:T(8,128)(2,1)S(1)}, u32[]{:S(2)}, u32[]{:S(2)}) %collective-permute-start.5) | collective-permute-done | bytes 262176 | tf_op jit(solution)/shard_map/ppermute | solution.py:229
  43.2 0.0 collective-permute-done.4.other_ref
  43.2 0.1 near.1
  43.3 1.5 %collective-permute-start.6 = (bf16[64,1024]{1,0:T(8,128)(2,1)S(1)}, bf16[64,1024]{1,0:T(8,128)(2,1)S(1)}, u32[]{:S(2)}, u32[]{:S(2)}) collective-permute-start(bf16[64,1024]{1,0:T(8,128)(2,1)S(1)} %get-tuple-element.26), channel_id=1, source_target_pairs={{0,8},{1,9},{2,10},{3,11},{4,12},{5,13},{6,14},{7,15},{8,0},{9,1},... | collective-permute-start | bytes 393224 | tf_op jit(solution)/shard_map/ppermute | solution.py:235
  44.8 0.0 collective-permute-start.7
  44.8 4.5 %collective-permute-done.1.across_ref = bf16[2,64,1024]{2,1,0:T(8,128)(2,1)S(1)} collective-permute-done((bf16[2,64,1024]{2,1,0:T(8,128)(2,1)S(1)}, bf16[2,64,1024]{2,1,0:T(8,128)(2,1)S(1)}, u32[]{:S(2)}, u32[]{:S(2)}) %collective-permute-start.1) | collective-permute-done | bytes 262176 | tf_op jit(solution)/shard_map/ppermute | solution.py:232
  49.3 0.0 collective-permute-done.2.other_ref
  49.4 0.6 collective-permute-start.8
  49.9 1.3 %collective-permute-done.6 = bf16[64,1024]{1,0:T(8,128)(2,1)S(1)} collective-permute-done((bf16[64,1024]{1,0:T(8,128)(2,1)S(1)}, bf16[64,1024]{1,0:T(8,128)(2,1)S(1)}, u32[]{:S(2)}, u32[]{:S(2)}) %collective-permute-start.6) | collective-permute-done | bytes 131104 | tf_op jit(solution)/shard_map/ppermute | solution.py:235
  51.2 1.4 %collective-permute-done.7 = bf16[64,1024]{1,0:T(8,128)(2,1)S(1)} collective-permute-done((bf16[64,1024]{1,0:T(8,128)(2,1)S(1)}, bf16[64,1024]{1,0:T(8,128)(2,1)S(1)}, u32[]{:S(2)}, u32[]{:S(2)}) %collective-permute-start.7) | collective-permute-done | bytes 131104 | tf_op jit(solution)/shard_map/ppermute | solution.py:235
  52.6 1.9 %collective-permute-done.8 = bf16[64,1024]{1,0:T(8,128)(2,1)S(1)} collective-permute-done((bf16[64,1024]{1,0:T(8,128)(2,1)S(1)}, bf16[64,1024]{1,0:T(8,128)(2,1)S(1)}, u32[]{:S(2)}, u32[]{:S(2)}) %collective-permute-start.8) | collective-permute-done | bytes 131104 | tf_op jit(solution)/shard_map/ppermute | solution.py:239
  54.6 0.1 add_convert_fusion
  54.6 0.1 reshape.13
  54.7 12.7 %all_to_all.10 = bf16[16,4,1024]{2,1,0:T(4,128)(2,1)S(1)} all-to-all(bf16[16,4,1024]{2,1,0:T(4,128)(2,1)S(1)} %reshape.13), channel_id=1, replica_groups=mesh['row'=16,'tp'=16] {'row'}, dimensions={0} | all-to-all | bytes 262144 | tf_op jit(solution)/shard_map/all_to_all | solution.py:241
  67.4 0.7 %reshape.15 = bf16[1,8,8,1024]{3,2,1,0:T(8,128)(2,1)} reshape(bf16[8,2,4,1024]{3,2,1,0:T(4,128)(2,1)S(1)} %bitcast.33) | data formatting | bytes 262144 | tf_op jit(solution)/shard_map/reshape | solution.py:242
  (6 shorter events, 0.2 us)
Async XLA Ops:
  0.0 27.8 %copy-start = (bf16[3,256,1024]{2,1,0:T(8,128)(2,1)S(1)}, bf16[3,256,1024]{2,1,0:T(8,128)(2,1)}, u32[]{:S(2)}) copy-start(bf16[3,256,1024]{2,1,0:T(8,128)(2,1)} %unite_ref.7) | copy-start | bytes 4718596
  0.0 1.2 %copy-start.2 = (bf16[1,8,128,256]{3,2,1,0:T(8,128)(2,1)S(1)}, bf16[1,8,128,256]{3,2,1,0:T(8,128)(2,1)}, u32[]{:S(2)}) copy-start(bf16[1,8,128,256]{3,2,1,0:T(8,128)(2,1)} %param.4) | copy-start | bytes 1572868
  1.2 26.6 %copy-start.3 = (f32[3,256]{1,0:T(4,128)S(1)}, f32[3,256]{1,0:T(4,128)}, u32[]{:S(2)}) copy-start(f32[3,256]{1,0:T(4,128)} %bias_ref.7) | copy-start | bytes 9220
  2.1 25.3 %all-to-all-start = ((bf16[16,64,256]{2,1,0:T(8,128)(2,1)}), bf16[16,64,256]{2,1,0:T(8,128)(2,1)S(1)}, u32[]{:S(2)}, u32[]{:S(2)}) async-start(bf16[16,64,256]{2,1,0:T(8,128)(2,1)} %pack.1), calls=%async_computation | async-start | bytes 1048576 | tf_op jit(solution)/shard_map/all_to_all | solution.py:216
  11.8 1.2 %copy-start.1 = (bf16[3,4,64,576]{3,2,1,0:T(8,128)(2,1)S(1)}, bf16[3,4,64,576]{3,2,1,0:T(8,128)(2,1)}, u32[]{:S(2)}) copy-start(bf16[3,4,64,576]{3,2,1,0:T(8,128)(2,1)} %param.5) | copy-start | bytes 2654212
  30.2 3.1 %collective-permute-start.3 = (bf16[2,64,1024]{2,1,0:T(8,128)(2,1)S(1)}, bf16[2,64,1024]{2,1,0:T(8,128)(2,1)S(1)}, u32[]{:S(2)}, u32[]{:S(2)}) collective-permute-start(bf16[2,64,1024]{2,1,0:T(8,128)(2,1)S(1)} %get-tuple-element.23), channel_id=1, source_target_pairs={{0,1},{1,0},{2,3},{3,2},{4,5},{5,4},{6,7},{7,6},{8,9},{9,8},{10,11... | collective-permute-start | bytes 786440 | tf_op jit(solution)/shard_map/ppermute | solution.py:225
  32.8 6.2 %collective-permute-start = (bf16[2,64,1024]{2,1,0:T(8,128)(2,1)S(1)}, bf16[2,64,1024]{2,1,0:T(8,128)(2,1)S(1)}, u32[]{:S(2)}, u32[]{:S(2)}) collective-permute-start(bf16[2,64,1024]{2,1,0:T(8,128)(2,1)S(1)} %get-tuple-element.18), channel_id=1, source_target_pairs={{0,1},{1,0},{2,3},{3,2},{4,5},{5,4},{6,7},{7,6},{8,9},{9,8},{10,11... | collective-permute-start | bytes 786440 | tf_op jit(solution)/shard_map/ppermute | solution.py:225
  33.4 9.8 %collective-permute-start.5 = (bf16[2,64,1024]{2,1,0:T(8,128)(2,1)S(1)}, bf16[2,64,1024]{2,1,0:T(8,128)(2,1)S(1)}, u32[]{:S(2)}, u32[]{:S(2)}) collective-permute-start(bf16[2,64,1024]{2,1,0:T(8,128)(2,1)S(1)} %far.3.refs_0_), channel_id=1, source_target_pairs={{0,2},{1,3},{2,0},{3,1},{4,6},{5,7},{6,4},{7,5},{8,10},{9,11},{10,... | collective-permute-start | bytes 786440 | tf_op jit(solution)/shard_map/ppermute | solution.py:229
  38.8 4.4 %collective-permute-start.4 = (bf16[2,64,1024]{2,1,0:T(8,128)(2,1)S(1)}, bf16[2,64,1024]{2,1,0:T(8,128)(2,1)S(1)}, u32[]{:S(2)}, u32[]{:S(2)}) collective-permute-start(bf16[2,64,1024]{2,1,0:T(8,128)(2,1)S(1)} %get-tuple-element.25), channel_id=1, source_target_pairs={{0,1},{1,0},{2,3},{3,2},{4,5},{5,4},{6,7},{7,6},{8,9},{9,8},{10,11... | collective-permute-start | bytes 786440 | tf_op jit(solution)/shard_map/ppermute | solution.py:225
  39.0 10.3 %collective-permute-start.1 = (bf16[2,64,1024]{2,1,0:T(8,128)(2,1)S(1)}, bf16[2,64,1024]{2,1,0:T(8,128)(2,1)S(1)}, u32[]{:S(2)}, u32[]{:S(2)}) collective-permute-start(bf16[2,64,1024]{2,1,0:T(8,128)(2,1)S(1)} %far.2.refs_0_), channel_id=1, source_target_pairs={{0,2},{1,3},{2,0},{3,1},{4,6},{5,7},{6,4},{7,5},{8,10},{9,11},{10,... | collective-permute-start | bytes 786440 | tf_op jit(solution)/shard_map/ppermute | solution.py:232
  42.1 7.2 %collective-permute-start.2 = (bf16[2,64,1024]{2,1,0:T(8,128)(2,1)S(1)}, bf16[2,64,1024]{2,1,0:T(8,128)(2,1)S(1)}, u32[]{:S(2)}, u32[]{:S(2)}) collective-permute-start(bf16[2,64,1024]{2,1,0:T(8,128)(2,1)S(1)} %get-tuple-element.20), channel_id=1, source_target_pairs={{0,1},{1,0},{2,3},{3,2},{4,5},{5,4},{6,7},{7,6},{8,9},{9,8},{10,11... | collective-permute-start | bytes 786440 | tf_op jit(solution)/shard_map/ppermute | solution.py:225
  43.3 7.9 %collective-permute-start.6 = (bf16[64,1024]{1,0:T(8,128)(2,1)S(1)}, bf16[64,1024]{1,0:T(8,128)(2,1)S(1)}, u32[]{:S(2)}, u32[]{:S(2)}) collective-permute-start(bf16[64,1024]{1,0:T(8,128)(2,1)S(1)} %get-tuple-element.26), channel_id=1, source_target_pairs={{0,8},{1,9},{2,10},{3,11},{4,12},{5,13},{6,14},{7,15},{8,0},{9,1},... | collective-permute-start | bytes 393224 | tf_op jit(solution)/shard_map/ppermute | solution.py:235
  44.8 7.8 %collective-permute-start.7 = (bf16[64,1024]{1,0:T(8,128)(2,1)S(1)}, bf16[64,1024]{1,0:T(8,128)(2,1)S(1)}, u32[]{:S(2)}, u32[]{:S(2)}) collective-permute-start(bf16[64,1024]{1,0:T(8,128)(2,1)S(1)} %get-tuple-element.27), channel_id=1, source_target_pairs={{0,12},{1,13},{2,14},{3,15},{4,0},{5,1},{6,2},{7,3},{8,4},{9,5},{1... | collective-permute-start | bytes 393224 | tf_op jit(solution)/shard_map/ppermute | solution.py:235
  49.4 5.2 %collective-permute-start.8 = (bf16[64,1024]{1,0:T(8,128)(2,1)S(1)}, bf16[64,1024]{1,0:T(8,128)(2,1)S(1)}, u32[]{:S(2)}, u32[]{:S(2)}) collective-permute-start(bf16[64,1024]{1,0:T(8,128)(2,1)S(1)} %get-tuple-element.28), channel_id=1, source_target_pairs={{0,4},{1,5},{2,6},{3,7},{4,8},{5,9},{6,10},{7,11},{8,12},{9,13},{1... | collective-permute-start | bytes 393224 | tf_op jit(solution)/shard_map/ppermute | solution.py:239

commit v5 on v4

--- a/solution.py
+++ b/solution.py
@@ -45,7 +45,7 @@
         pack_kernel,
         out_specs=VMEM_SPEC,
         out_shape=pltpu.VMEM((16, PIXELS, x.shape[2]), jnp.bfloat16),
-        compiler_params=pltpu.CompilerParams(vmem_limit_bytes=16 * 2**20),
+        compiler_params=pltpu.CompilerParams(vmem_limit_bytes=60 * 2**20),
         name="pack",
     )(x)
 
@@ -195,6 +195,23 @@
     )(spots, spread_x, wide, bias, unite, *after)
 
 
+def finish_kernel(x_ref, out_ref):
+    for j in range(8):
+        halves = [x_ref[8 * side + j].astype(jnp.float32) for side in range(2)]
+        out_ref[j] = jnp.concatenate(halves, axis=0).astype(jnp.bfloat16)
+
+
+def finish(bands):
+    return pl.pallas_call(
+        finish_kernel,
+        in_specs=[VMEM_SPEC],
+        out_specs=VMEM_SPEC,
+        out_shape=jax.ShapeDtypeStruct((8, 2 * LOW, bands.shape[2]), jnp.bfloat16),
+        compiler_params=pltpu.CompilerParams(vmem_limit_bytes=16 * 2**20),
+        name="finish",
+    )(bands)
+
+
 CHUNKS = (((2, 1), (3, 1)), ((1, 1), (0, 1)), ((2, 0), (3, 0)), ((1, 0), (0, 0)))
 SWAP = [(i, i ^ 1) for i in range(16)]
 FAR = [(i, i ^ 2) for i in range(16)]
@@ -239,7 +256,7 @@
     previous = lax.ppermute(previous, "tp", hop(1))
     result = added(own, opposite, following, previous).astype(jnp.bfloat16)
     bands = lax.all_to_all(result.reshape(BANDS, LOW, width), "row", 0, 0)
-    return bands.reshape(2, 8, LOW, width).transpose(1, 0, 2, 3).reshape(1, 8, 8, width)
+    return finish(bands)[None]
 
 
 def solution(mesh):

time: 69.1 us -> 69 us (level)
  Pallas kernels: 12 us -> 13.9 us
  local copies, waits for them, and re-layouts: 3.16 us -> 1.26 us
    unnamed x8 -> x6, local copies, waits for them, and re-layouts: 2.36 us -> 1.2 us
    pallas_call x1, Pallas kernels: 0.93 us -> 2.08 us  [pack(): pl.pallas_call(pack_kernel, out_specs=VMEM_SPEC, out_shape=pltpu.VMEM((16...]
    reshape x2 -> x0, local copies, waits for them, and re-layouts: 0.74 us -> none  [on_device(): bands.reshape(2, 8, LOW, width).transpose(1, 0, 2, 3)]
where the time goes in v5:
time: 69 us; the launch traced here: 68 us
  waiting for transfers between devices  23.3 us (34%)
  starting transfers between devices  16.4 us (24%)
  Pallas kernels  13.9 us (20%)
  blocking collectives  12.7 us (18%)
  local copies, waits for them, and re-layouts  1.26 us (2%)
    all_to_all x1, waiting for transfers between devices, on_device(): mine = lax.all_to_all(packed, 'row', 0, 0)  13.4 us
    all_to_all x1, blocking collectives, on_device(): bands = lax.all_to_all(result.reshape(BANDS, LOW, width), 'row', 0, 0)  12.7 us
    pallas_call x4, Pallas kernels, head_terms(): pl.pallas_call(functools.partial(head_kernel, chunk), in_specs=[pl.BlockS...  9.73 us
    all_to_all x1, starting transfers between devices, on_device(): mine = lax.all_to_all(packed, 'row', 0, 0)  9.58 us
    ppermute x1, waiting for transfers between devices, on_device(): across1 = lax.ppermute(far1, 'tp', FAR)  4.45 us
    ppermute x1, starting transfers between devices, on_device(): across0 = lax.ppermute(far0, 'tp', FAR)  2.99 us
    pallas_call x1, Pallas kernels, pack(): pl.pallas_call(pack_kernel, out_specs=VMEM_SPEC, out_shape=pltpu.VMEM((16...  2.08 us
    ppermute x1, waiting for transfers between devices, on_device(): previous = lax.ppermute(previous, 'tp', hop(1))  1.93 us
  transfers between devices with their start and end apart: 10, of which 6 were waited for; matrix products, arithmetic and copies ran while one was open for 0% of the time, Pallas kernels for 12%

profile of v5, /device:TPU:6, one launch (start us, length us, event | category | flops | bytes accessed | tf_op | source)
XLA Modules:
  0.0 68.0 jit_solution(15245895207650181925)
XLA Ops:
  0.0 0.0 copy-start
  0.0 0.0 copy-start.2
  0.0 2.1 %pack.1 = bf16[16,64,256]{2,1,0:T(8,128)(2,1)} custom-call(bf16[8,128,256]{2,1,0:T(8,128)(2,1)} %bitcast.28), custom_call_target="tpu_custom_call" | custom-call | tf_op jit(solution)/shard_map/pack/pallas_call | solution.py:44
  2.1 9.6 %all-to-all-start = ((bf16[16,64,256]{2,1,0:T(8,128)(2,1)}), bf16[16,64,256]{2,1,0:T(8,128)(2,1)S(1)}, u32[]{:S(2)}, u32[]{:S(2)}) async-start(bf16[16,64,256]{2,1,0:T(8,128)(2,1)} %pack.1), calls=%async_computation | async-start | bytes 1048576 | tf_op jit(solution)/shard_map/all_to_all | solution.py:233
  11.8 0.0 copy-start.1
  11.9 1.2 %copy-done.1 = bf16[3,4,64,576]{3,2,1,0:T(8,128)(2,1)S(1)} copy-done((bf16[3,4,64,576]{3,2,1,0:T(8,128)(2,1)S(1)}, bf16[3,4,64,576]{3,2,1,0:T(8,128)(2,1)}, u32[]{:S(2)}) %copy-start.1) | copy-done | bytes 884760
  13.0 0.7 %turn.1.w_ref = bf16[3,576,256]{2,1,0:T(8,128)(2,1)S(1)} custom-call(bf16[3,256,576]{2,1,0:T(8,128)(2,1)S(1)} %bitcast.27), custom_call_target="tpu_custom_call" | custom-call | tf_op jit(solution)/shard_map/turn/pallas_call | solution.py:66
  13.8 0.1 add_bitcast_fusion
  13.9 0.1 add_bitcast_fusion.2
  14.0 13.4 %all-to-all-done.x_ref = bf16[16,64,256]{2,1,0:T(8,128)(2,1)S(1)} async-done(((bf16[16,64,256]{2,1,0:T(8,128)(2,1)}), bf16[16,64,256]{2,1,0:T(8,128)(2,1)S(1)}, u32[]{:S(2)}, u32[]{:S(2)}) %all-to-all-start) | async-done | bytes 524320 | tf_op jit(solution)/shard_map/all_to_all | solution.py:233
  27.4 0.4 spread.1.s_ref
  27.7 0.0 copy-done
  27.8 0.0 copy-done.2
  27.8 2.4 %head.6 = (bf16[2,64,1024]{2,1,0:T(8,128)(2,1)S(1)}, f32[2,64,1024]{2,1,0:T(8,128)S(1)}) custom-call(s32[4,4]{1,0:T(4,128)S(1)} %pad_add_fusion.spot_ref, bf16[7,24,64,256]{3,2,1,0:T(8,128)(2,1)S(1)} %spread.1.s_ref, bf16[3,576,256]{2,1,0:T(8,128)(2,1)S(1)} %turn.1.w_ref, f32[3,256]{1,0:T(4,128)S(1)} %copy-done.2, bf16[3,256,1024]{2,1,0:T(8,128)(2,1)S(1)} %copy-done), custom_call_target="tpu_custom_call" | custom-call | tf_op jit(solution)/shard_map/head/pallas_call | solution.py:188
  30.2 0.1 collective-permute-start.3
  30.3 2.4 %head.4 = (bf16[2,64,1024]{2,1,0:T(8,128)(2,1)S(1)}, f32[2,64,1024]{2,1,0:T(8,128)S(1)}) custom-call(s32[4,4]{1,0:T(4,128)S(1)} %pad_add_fusion.spot_ref, bf16[7,24,64,256]{3,2,1,0:T(8,128)(2,1)S(1)} %spread.1.s_ref, bf16[3,576,256]{2,1,0:T(8,128)(2,1)S(1)} %turn.1.w_ref, f32[3,256]{1,0:T(4,128)S(1)} %copy-done.2, bf16[3,256,1024]{2,1,0:T(8,128)(2,1)S(1)} %copy-done), custom_call_target="tpu_custom_call" | custom-call | tf_op jit(solution)/shard_map/head/pallas_call | solution.py:188
  32.7 0.6 collective-permute-start
  33.3 0.0 collective-permute-done.3.other_ref
  33.4 3.0 %collective-permute-start.5 = (bf16[2,64,1024]{2,1,0:T(8,128)(2,1)S(1)}, bf16[2,64,1024]{2,1,0:T(8,128)(2,1)S(1)}, u32[]{:S(2)}, u32[]{:S(2)}) collective-permute-start(bf16[2,64,1024]{2,1,0:T(8,128)(2,1)S(1)} %far.3.refs_0_), channel_id=1, source_target_pairs={{0,2},{1,3},{2,0},{3,1},{4,6},{5,7},{6,4},{7,5},{8,10},{9,11},{10,... | collective-permute-start | bytes 786440 | tf_op jit(solution)/shard_map/ppermute | solution.py:246
  36.4 2.4 %head.7 = (bf16[2,64,1024]{2,1,0:T(8,128)(2,1)S(1)}, f32[2,64,1024]{2,1,0:T(8,128)S(1)}) custom-call(s32[4,4]{1,0:T(4,128)S(1)} %pad_add_fusion.spot_ref, bf16[7,24,64,256]{3,2,1,0:T(8,128)(2,1)S(1)} %spread.1.s_ref, bf16[3,576,256]{2,1,0:T(8,128)(2,1)S(1)} %turn.1.w_ref, f32[3,256]{1,0:T(4,128)S(1)} %copy-done.2, bf16[3,256,1024]{2,1,0:T(8,128)(2,1)S(1)} %copy-done, ...), custom_call_target="tpu_custom_call" | custom-call | tf_op jit(solution)/shard_map/head/pallas_call | solution.py:188
  38.8 0.1 collective-permute-start.4
  38.9 0.0 collective-permute-done.other_ref
  39.0 0.7 %collective-permute-start.1 = (bf16[2,64,1024]{2,1,0:T(8,128)(2,1)S(1)}, bf16[2,64,1024]{2,1,0:T(8,128)(2,1)S(1)}, u32[]{:S(2)}, u32[]{:S(2)}) collective-permute-start(bf16[2,64,1024]{2,1,0:T(8,128)(2,1)S(1)} %far.2.refs_0_), channel_id=1, source_target_pairs={{0,2},{1,3},{2,0},{3,1},{4,6},{5,7},{6,4},{7,5},{8,10},{9,11},{10,... | collective-permute-start | bytes 786440 | tf_op jit(solution)/shard_map/ppermute | solution.py:249
  39.7 2.4 %head.5 = (bf16[2,64,1024]{2,1,0:T(8,128)(2,1)S(1)}, f32[2,64,1024]{2,1,0:T(8,128)S(1)}) custom-call(s32[4,4]{1,0:T(4,128)S(1)} %pad_add_fusion.spot_ref, bf16[7,24,64,256]{3,2,1,0:T(8,128)(2,1)S(1)} %spread.1.s_ref, bf16[3,576,256]{2,1,0:T(8,128)(2,1)S(1)} %turn.1.w_ref, f32[3,256]{1,0:T(4,128)S(1)} %copy-done.2, bf16[3,256,1024]{2,1,0:T(8,128)(2,1)S(1)} %copy-done, ...), custom_call_target="tpu_custom_call" | custom-call | tf_op jit(solution)/shard_map/head/pallas_call | solution.py:188
  42.1 0.3 collective-permute-start.2
  42.4 0.8 %collective-permute-done.5.across_ref = bf16[2,64,1024]{2,1,0:T(8,128)(2,1)S(1)} collective-permute-done((bf16[2,64,1024]{2,1,0:T(8,128)(2,1)S(1)}, bf16[2,64,1024]{2,1,0:T(8,128)(2,1)S(1)}, u32[]{:S(2)}, u32[]{:S(2)}) %collective-permute-start.5) | collective-permute-done | bytes 262176 | tf_op jit(solution)/shard_map/ppermute | solution.py:246
  43.2 0.0 collective-permute-done.4.other_ref
  43.2 0.1 near.1
  43.3 1.5 %collective-permute-start.6 = (bf16[64,1024]{1,0:T(8,128)(2,1)S(1)}, bf16[64,1024]{1,0:T(8,128)(2,1)S(1)}, u32[]{:S(2)}, u32[]{:S(2)}) collective-permute-start(bf16[64,1024]{1,0:T(8,128)(2,1)S(1)} %get-tuple-element.26), channel_id=1, source_target_pairs={{0,8},{1,9},{2,10},{3,11},{4,12},{5,13},{6,14},{7,15},{8,0},{9,1},... | collective-permute-start | bytes 393224 | tf_op jit(solution)/shard_map/ppermute | solution.py:252
  44.8 0.0 collective-permute-start.7
  44.8 4.5 %collective-permute-done.1.across_ref = bf16[2,64,1024]{2,1,0:T(8,128)(2,1)S(1)} collective-permute-done((bf16[2,64,1024]{2,1,0:T(8,128)(2,1)S(1)}, bf16[2,64,1024]{2,1,0:T(8,128)(2,1)S(1)}, u32[]{:S(2)}, u32[]{:S(2)}) %collective-permute-start.1) | collective-permute-done | bytes 262176 | tf_op jit(solution)/shard_map/ppermute | solution.py:249
  49.3 0.0 collective-permute-done.2.other_ref
  49.4 0.6 collective-permute-start.8
  49.9 1.3 %collective-permute-done.6 = bf16[64,1024]{1,0:T(8,128)(2,1)S(1)} collective-permute-done((bf16[64,1024]{1,0:T(8,128)(2,1)S(1)}, bf16[64,1024]{1,0:T(8,128)(2,1)S(1)}, u32[]{:S(2)}, u32[]{:S(2)}) %collective-permute-start.6) | collective-permute-done | bytes 131104 | tf_op jit(solution)/shard_map/ppermute | solution.py:252
  51.2 1.4 %collective-permute-done.7 = bf16[64,1024]{1,0:T(8,128)(2,1)S(1)} collective-permute-done((bf16[64,1024]{1,0:T(8,128)(2,1)S(1)}, bf16[64,1024]{1,0:T(8,128)(2,1)S(1)}, u32[]{:S(2)}, u32[]{:S(2)}) %collective-permute-start.7) | collective-permute-done | bytes 131104 | tf_op jit(solution)/shard_map/ppermute | solution.py:252
  52.6 1.9 %collective-permute-done.8 = bf16[64,1024]{1,0:T(8,128)(2,1)S(1)} collective-permute-done((bf16[64,1024]{1,0:T(8,128)(2,1)S(1)}, bf16[64,1024]{1,0:T(8,128)(2,1)S(1)}, u32[]{:S(2)}, u32[]{:S(2)}) %collective-permute-start.8) | collective-permute-done | bytes 131104 | tf_op jit(solution)/shard_map/ppermute | solution.py:256
  54.6 0.1 add_convert_fusion
  54.6 0.1 reshape.7
  54.7 12.7 %all_to_all.10.x_ref = bf16[16,4,1024]{2,1,0:T(4,128)(2,1)S(1)} all-to-all(bf16[16,4,1024]{2,1,0:T(4,128)(2,1)S(1)} %reshape.7), channel_id=1, replica_groups=mesh['row'=16,'tp'=16] {'row'}, dimensions={0} | all-to-all | bytes 262144 | tf_op jit(solution)/shard_map/all_to_all | solution.py:258
  67.4 0.7 %finish.1 = bf16[8,8,1024]{2,1,0:T(8,128)(2,1)} custom-call(bf16[16,4,1024]{2,1,0:T(4,128)(2,1)S(1)} %all_to_all.10.x_ref), custom_call_target="tpu_custom_call" | custom-call | tf_op jit(solution)/shard_map/finish/pallas_call | solution.py:205
  (5 shorter events, 0.2 us)
Async XLA Ops:
  0.0 27.8 %copy-start = (bf16[3,256,1024]{2,1,0:T(8,128)(2,1)S(1)}, bf16[3,256,1024]{2,1,0:T(8,128)(2,1)}, u32[]{:S(2)}) copy-start(bf16[3,256,1024]{2,1,0:T(8,128)(2,1)} %unite_ref.7) | copy-start | bytes 4718596
  0.0 27.8 %copy-start.2 = (f32[3,256]{1,0:T(4,128)S(1)}, f32[3,256]{1,0:T(4,128)}, u32[]{:S(2)}) copy-start(f32[3,256]{1,0:T(4,128)} %bias_ref.7) | copy-start | bytes 9220
  2.1 25.3 %all-to-all-start = ((bf16[16,64,256]{2,1,0:T(8,128)(2,1)}), bf16[16,64,256]{2,1,0:T(8,128)(2,1)S(1)}, u32[]{:S(2)}, u32[]{:S(2)}) async-start(bf16[16,64,256]{2,1,0:T(8,128)(2,1)} %pack.1), calls=%async_computation | async-start | bytes 1048576 | tf_op jit(solution)/shard_map/all_to_all | solution.py:233
  11.8 1.2 %copy-start.1 = (bf16[3,4,64,576]{3,2,1,0:T(8,128)(2,1)S(1)}, bf16[3,4,64,576]{3,2,1,0:T(8,128)(2,1)}, u32[]{:S(2)}) copy-start(bf16[3,4,64,576]{3,2,1,0:T(8,128)(2,1)} %param.5) | copy-start | bytes 2654212
  30.2 3.1 %collective-permute-start.3 = (bf16[2,64,1024]{2,1,0:T(8,128)(2,1)S(1)}, bf16[2,64,1024]{2,1,0:T(8,128)(2,1)S(1)}, u32[]{:S(2)}, u32[]{:S(2)}) collective-permute-start(bf16[2,64,1024]{2,1,0:T(8,128)(2,1)S(1)} %get-tuple-element.23), channel_id=1, source_target_pairs={{0,1},{1,0},{2,3},{3,2},{4,5},{5,4},{6,7},{7,6},{8,9},{9,8},{10,11... | collective-permute-start | bytes 786440 | tf_op jit(solution)/shard_map/ppermute | solution.py:242
  32.7 6.2 %collective-permute-start = (bf16[2,64,1024]{2,1,0:T(8,128)(2,1)S(1)}, bf16[2,64,1024]{2,1,0:T(8,128)(2,1)S(1)}, u32[]{:S(2)}, u32[]{:S(2)}) collective-permute-start(bf16[2,64,1024]{2,1,0:T(8,128)(2,1)S(1)} %get-tuple-element.18), channel_id=1, source_target_pairs={{0,1},{1,0},{2,3},{3,2},{4,5},{5,4},{6,7},{7,6},{8,9},{9,8},{10,11... | collective-permute-start | bytes 786440 | tf_op jit(solution)/shard_map/ppermute | solution.py:242
  33.4 9.8 %collective-permute-start.5 = (bf16[2,64,1024]{2,1,0:T(8,128)(2,1)S(1)}, bf16[2,64,1024]{2,1,0:T(8,128)(2,1)S(1)}, u32[]{:S(2)}, u32[]{:S(2)}) collective-permute-start(bf16[2,64,1024]{2,1,0:T(8,128)(2,1)S(1)} %far.3.refs_0_), channel_id=1, source_target_pairs={{0,2},{1,3},{2,0},{3,1},{4,6},{5,7},{6,4},{7,5},{8,10},{9,11},{10,... | collective-permute-start | bytes 786440 | tf_op jit(solution)/shard_map/ppermute | solution.py:246
  38.8 4.4 %collective-permute-start.4 = (bf16[2,64,1024]{2,1,0:T(8,128)(2,1)S(1)}, bf16[2,64,1024]{2,1,0:T(8,128)(2,1)S(1)}, u32[]{:S(2)}, u32[]{:S(2)}) collective-permute-start(bf16[2,64,1024]{2,1,0:T(8,128)(2,1)S(1)} %get-tuple-element.25), channel_id=1, source_target_pairs={{0,1},{1,0},{2,3},{3,2},{4,5},{5,4},{6,7},{7,6},{8,9},{9,8},{10,11... | collective-permute-start | bytes 786440 | tf_op jit(solution)/shard_map/ppermute | solution.py:242
  39.0 10.3 %collective-permute-start.1 = (bf16[2,64,1024]{2,1,0:T(8,128)(2,1)S(1)}, bf16[2,64,1024]{2,1,0:T(8,128)(2,1)S(1)}, u32[]{:S(2)}, u32[]{:S(2)}) collective-permute-start(bf16[2,64,1024]{2,1,0:T(8,128)(2,1)S(1)} %far.2.refs_0_), channel_id=1, source_target_pairs={{0,2},{1,3},{2,0},{3,1},{4,6},{5,7},{6,4},{7,5},{8,10},{9,11},{10,... | collective-permute-start | bytes 786440 | tf_op jit(solution)/shard_map/ppermute | solution.py:249
  42.1 7.2 %collective-permute-start.2 = (bf16[2,64,1024]{2,1,0:T(8,128)(2,1)S(1)}, bf16[2,64,1024]{2,1,0:T(8,128)(2,1)S(1)}, u32[]{:S(2)}, u32[]{:S(2)}) collective-permute-start(bf16[2,64,1024]{2,1,0:T(8,128)(2,1)S(1)} %get-tuple-element.20), channel_id=1, source_target_pairs={{0,1},{1,0},{2,3},{3,2},{4,5},{5,4},{6,7},{7,6},{8,9},{9,8},{10,11... | collective-permute-start | bytes 786440 | tf_op jit(solution)/shard_map/ppermute | solution.py:242
  43.3 7.9 %collective-permute-start.6 = (bf16[64,1024]{1,0:T(8,128)(2,1)S(1)}, bf16[64,1024]{1,0:T(8,128)(2,1)S(1)}, u32[]{:S(2)}, u32[]{:S(2)}) collective-permute-start(bf16[64,1024]{1,0:T(8,128)(2,1)S(1)} %get-tuple-element.26), channel_id=1, source_target_pairs={{0,8},{1,9},{2,10},{3,11},{4,12},{5,13},{6,14},{7,15},{8,0},{9,1},... | collective-permute-start | bytes 393224 | tf_op jit(solution)/shard_map/ppermute | solution.py:252
  44.8 7.8 %collective-permute-start.7 = (bf16[64,1024]{1,0:T(8,128)(2,1)S(1)}, bf16[64,1024]{1,0:T(8,128)(2,1)S(1)}, u32[]{:S(2)}, u32[]{:S(2)}) collective-permute-start(bf16[64,1024]{1,0:T(8,128)(2,1)S(1)} %get-tuple-element.27), channel_id=1, source_target_pairs={{0,12},{1,13},{2,14},{3,15},{4,0},{5,1},{6,2},{7,3},{8,4},{9,5},{1... | collective-permute-start | bytes 393224 | tf_op jit(solution)/shard_map/ppermute | solution.py:252
  49.4 5.2 %collective-permute-start.8 = (bf16[64,1024]{1,0:T(8,128)(2,1)S(1)}, bf16[64,1024]{1,0:T(8,128)(2,1)S(1)}, u32[]{:S(2)}, u32[]{:S(2)}) collective-permute-start(bf16[64,1024]{1,0:T(8,128)(2,1)S(1)} %get-tuple-element.28), channel_id=1, source_target_pairs={{0,4},{1,5},{2,6},{3,7},{4,8},{5,9},{6,10},{7,11},{8,12},{9,13},{1... | collective-permute-start | bytes 393224 | tf_op jit(solution)/shard_map/ppermute | solution.py:256

commit v6 on v4

--- a/solution.py
+++ b/solution.py
@@ -211,7 +211,7 @@
         jnp.stack([4 * ((chip_x + ahead) % 4) + 2 * ((chip_y + across) % 2) + (core + side) % 2 for side in (1, 0) for ahead, across in chunk])
         for chunk in CHUNKS
     ])
-    packed = pack(feature_map[0])
+    packed, unite_weight = lax.optimization_barrier((pack(feature_map[0]), unite_weight))
     wide = in_vmem(turn(conv_weight))
     mine = lax.all_to_all(packed, "row", 0, 0)
     spread_x = spread(mine)

time: 69.1 us -> 69.1 us (level)
  no operation moved by 1% of the time
where the time goes in v6:
time: 69.1 us; the launch traced here: 68.1 us
  waiting for transfers between devices  23.3 us (34%)
  starting transfers between devices  16.4 us (24%)
  blocking collectives  12.7 us (18%)
  Pallas kernels  12 us (17%)
  local copies, waits for them, and re-layouts  3.16 us (5%)
    all_to_all x1, waiting for transfers between devices, on_device(): mine = lax.all_to_all(packed, 'row', 0, 0)  13.4 us
    all_to_all x1, blocking collectives, on_device(): bands = lax.all_to_all(result.reshape(BANDS, LOW, width), 'row', 0, 0)  12.7 us
    pallas_call x4, Pallas kernels, head_terms(): pl.pallas_call(functools.partial(head_kernel, chunk), in_specs=[pl.BlockS...  9.73 us
    all_to_all x1, starting transfers between devices, on_device(): mine = lax.all_to_all(packed, 'row', 0, 0)  9.58 us
    ppermute x1, waiting for transfers between devices, on_device(): across1 = lax.ppermute(far1, 'tp', FAR)  4.46 us
    ppermute x1, starting transfers between devices, on_device(): across0 = lax.ppermute(far0, 'tp', FAR)  2.99 us
    unnamed x8, local copies, waits for them, and re-layouts  2.36 us
    ppermute x1, waiting for transfers between devices, on_device(): previous = lax.ppermute(previous, 'tp', hop(1))  1.93 us
  transfers between devices with their start and end apart: 10, of which 6 were waited for; matrix products, arithmetic and copies ran while one was open for 0% of the time, Pallas kernels for 12%

profile of v6, /device:TPU:6, one launch (start us, length us, event | category | flops | bytes accessed | tf_op | source)
XLA Modules:
  0.0 68.1 jit_solution(8068364678074542560)
XLA Ops:
  0.0 0.0 copy-start
  0.0 0.0 copy-start.2
  0.0 1.2 %copy-done.2 = bf16[1,8,128,256]{3,2,1,0:T(8,128)(2,1)S(1)} copy-done((bf16[1,8,128,256]{3,2,1,0:T(8,128)(2,1)S(1)}, bf16[1,8,128,256]{3,2,1,0:T(8,128)(2,1)}, u32[]{:S(2)}) %copy-start.2) | copy-done | bytes 524312
  1.2 0.0 copy-start.3
  1.2 0.9 %pack.1 = bf16[16,64,256]{2,1,0:T(8,128)(2,1)} custom-call(bf16[8,128,256]{2,1,0:T(8,128)(2,1)S(1)} %bitcast.31), custom_call_target="tpu_custom_call" | custom-call | tf_op jit(solution)/shard_map/pack/pallas_call | solution.py:44
  2.1 9.6 %all-to-all-start = ((bf16[16,64,256]{2,1,0:T(8,128)(2,1)}), bf16[16,64,256]{2,1,0:T(8,128)(2,1)S(1)}, u32[]{:S(2)}, u32[]{:S(2)}) async-start(bf16[16,64,256]{2,1,0:T(8,128)(2,1)} %pack.1), calls=%async_computation | async-start | bytes 1048576 | tf_op jit(solution)/shard_map/all_to_all | solution.py:216
  11.8 0.0 copy-start.1
  11.9 1.2 %copy-done.1 = bf16[3,4,64,576]{3,2,1,0:T(8,128)(2,1)S(1)} copy-done((bf16[3,4,64,576]{3,2,1,0:T(8,128)(2,1)S(1)}, bf16[3,4,64,576]{3,2,1,0:T(8,128)(2,1)}, u32[]{:S(2)}) %copy-start.1) | copy-done | bytes 884760
  13.0 0.7 %turn.1.w_ref = bf16[3,576,256]{2,1,0:T(8,128)(2,1)S(1)} custom-call(bf16[3,256,576]{2,1,0:T(8,128)(2,1)S(1)} %bitcast.30), custom_call_target="tpu_custom_call" | custom-call | tf_op jit(solution)/shard_map/turn/pallas_call | solution.py:66
  13.8 0.1 add_bitcast_fusion
  13.9 0.1 add_bitcast_fusion.2
  14.0 13.4 %all-to-all-done.x_ref = bf16[16,64,256]{2,1,0:T(8,128)(2,1)S(1)} async-done(((bf16[16,64,256]{2,1,0:T(8,128)(2,1)}), bf16[16,64,256]{2,1,0:T(8,128)(2,1)S(1)}, u32[]{:S(2)}, u32[]{:S(2)}) %all-to-all-start) | async-done | bytes 524320 | tf_op jit(solution)/shard_map/all_to_all | solution.py:216
  27.4 0.4 spread.1.s_ref
  27.8 0.0 copy-done
  27.8 0.0 copy-done.3
  27.8 2.4 %head.6 = (bf16[2,64,1024]{2,1,0:T(8,128)(2,1)S(1)}, f32[2,64,1024]{2,1,0:T(8,128)S(1)}) custom-call(s32[4,4]{1,0:T(4,128)S(1)} %pad_add_fusion.spot_ref, bf16[7,24,64,256]{3,2,1,0:T(8,128)(2,1)S(1)} %spread.1.s_ref, bf16[3,576,256]{2,1,0:T(8,128)(2,1)S(1)} %turn.1.w_ref, f32[3,256]{1,0:T(4,128)S(1)} %copy-done.3, bf16[3,256,1024]{2,1,0:T(8,128)(2,1)S(1)} %copy-done), custom_call_target="tpu_custom_call" | custom-call | tf_op jit(solution)/shard_map/head/pallas_call | solution.py:188
  30.2 0.1 collective-permute-start.3
  30.3 2.4 %head.4 = (bf16[2,64,1024]{2,1,0:T(8,128)(2,1)S(1)}, f32[2,64,1024]{2,1,0:T(8,128)S(1)}) custom-call(s32[4,4]{1,0:T(4,128)S(1)} %pad_add_fusion.spot_ref, bf16[7,24,64,256]{3,2,1,0:T(8,128)(2,1)S(1)} %spread.1.s_ref, bf16[3,576,256]{2,1,0:T(8,128)(2,1)S(1)} %turn.1.w_ref, f32[3,256]{1,0:T(4,128)S(1)} %copy-done.3, bf16[3,256,1024]{2,1,0:T(8,128)(2,1)S(1)} %copy-done), custom_call_target="tpu_custom_call" | custom-call | tf_op jit(solution)/shard_map/head/pallas_call | solution.py:188
  32.8 0.6 collective-permute-start
  33.3 0.0 collective-permute-done.3.other_ref
  33.4 3.0 %collective-permute-start.5 = (bf16[2,64,1024]{2,1,0:T(8,128)(2,1)S(1)}, bf16[2,64,1024]{2,1,0:T(8,128)(2,1)S(1)}, u32[]{:S(2)}, u32[]{:S(2)}) collective-permute-start(bf16[2,64,1024]{2,1,0:T(8,128)(2,1)S(1)} %far.3.refs_0_), channel_id=1, source_target_pairs={{0,2},{1,3},{2,0},{3,1},{4,6},{5,7},{6,4},{7,5},{8,10},{9,11},{10,... | collective-permute-start | bytes 786440 | tf_op jit(solution)/shard_map/ppermute | solution.py:229
  36.4 2.4 %head.7 = (bf16[2,64,1024]{2,1,0:T(8,128)(2,1)S(1)}, f32[2,64,1024]{2,1,0:T(8,128)S(1)}) custom-call(s32[4,4]{1,0:T(4,128)S(1)} %pad_add_fusion.spot_ref, bf16[7,24,64,256]{3,2,1,0:T(8,128)(2,1)S(1)} %spread.1.s_ref, bf16[3,576,256]{2,1,0:T(8,128)(2,1)S(1)} %turn.1.w_ref, f32[3,256]{1,0:T(4,128)S(1)} %copy-done.3, bf16[3,256,1024]{2,1,0:T(8,128)(2,1)S(1)} %copy-done, ...), custom_call_target="tpu_custom_call" | custom-call | tf_op jit(solution)/shard_map/head/pallas_call | solution.py:188
  38.8 0.1 collective-permute-start.4
  38.9 0.0 collective-permute-done.other_ref
  39.0 0.7 %collective-permute-start.1 = (bf16[2,64,1024]{2,1,0:T(8,128)(2,1)S(1)}, bf16[2,64,1024]{2,1,0:T(8,128)(2,1)S(1)}, u32[]{:S(2)}, u32[]{:S(2)}) collective-permute-start(bf16[2,64,1024]{2,1,0:T(8,128)(2,1)S(1)} %far.2.refs_0_), channel_id=1, source_target_pairs={{0,2},{1,3},{2,0},{3,1},{4,6},{5,7},{6,4},{7,5},{8,10},{9,11},{10,... | collective-permute-start | bytes 786440 | tf_op jit(solution)/shard_map/ppermute | solution.py:232
  39.7 2.4 %head.5 = (bf16[2,64,1024]{2,1,0:T(8,128)(2,1)S(1)}, f32[2,64,1024]{2,1,0:T(8,128)S(1)}) custom-call(s32[4,4]{1,0:T(4,128)S(1)} %pad_add_fusion.spot_ref, bf16[7,24,64,256]{3,2,1,0:T(8,128)(2,1)S(1)} %spread.1.s_ref, bf16[3,576,256]{2,1,0:T(8,128)(2,1)S(1)} %turn.1.w_ref, f32[3,256]{1,0:T(4,128)S(1)} %copy-done.3, bf16[3,256,1024]{2,1,0:T(8,128)(2,1)S(1)} %copy-done, ...), custom_call_target="tpu_custom_call" | custom-call | tf_op jit(solution)/shard_map/head/pallas_call | solution.py:188
  42.1 0.3 collective-permute-start.2
  42.4 0.8 %collective-permute-done.5.across_ref = bf16[2,64,1024]{2,1,0:T(8,128)(2,1)S(1)} collective-permute-done((bf16[2,64,1024]{2,1,0:T(8,128)(2,1)S(1)}, bf16[2,64,1024]{2,1,0:T(8,128)(2,1)S(1)}, u32[]{:S(2)}, u32[]{:S(2)}) %collective-permute-start.5) | collective-permute-done | bytes 262176 | tf_op jit(solution)/shard_map/ppermute | solution.py:229
  43.2 0.0 collective-permute-done.4.other_ref
  43.2 0.1 near.1
  43.3 1.5 %collective-permute-start.6 = (bf16[64,1024]{1,0:T(8,128)(2,1)S(1)}, bf16[64,1024]{1,0:T(8,128)(2,1)S(1)}, u32[]{:S(2)}, u32[]{:S(2)}) collective-permute-start(bf16[64,1024]{1,0:T(8,128)(2,1)S(1)} %get-tuple-element.30), channel_id=1, source_target_pairs={{0,8},{1,9},{2,10},{3,11},{4,12},{5,13},{6,14},{7,15},{8,0},{9,1},... | collective-permute-start | bytes 393224 | tf_op jit(solution)/shard_map/ppermute | solution.py:235
  44.8 0.0 collective-permute-start.7
  44.8 4.5 %collective-permute-done.1.across_ref = bf16[2,64,1024]{2,1,0:T(8,128)(2,1)S(1)} collective-permute-done((bf16[2,64,1024]{2,1,0:T(8,128)(2,1)S(1)}, bf16[2,64,1024]{2,1,0:T(8,128)(2,1)S(1)}, u32[]{:S(2)}, u32[]{:S(2)}) %collective-permute-start.1) | collective-permute-done | bytes 262176 | tf_op jit(solution)/shard_map/ppermute | solution.py:232
  49.3 0.0 collective-permute-done.2.other_ref
  49.4 0.6 collective-permute-start.8
  49.9 1.3 %collective-permute-done.6 = bf16[64,1024]{1,0:T(8,128)(2,1)S(1)} collective-permute-done((bf16[64,1024]{1,0:T(8,128)(2,1)S(1)}, bf16[64,1024]{1,0:T(8,128)(2,1)S(1)}, u32[]{:S(2)}, u32[]{:S(2)}) %collective-permute-start.6) | collective-permute-done | bytes 131104 | tf_op jit(solution)/shard_map/ppermute | solution.py:235
  51.2 1.4 %collective-permute-done.7 = bf16[64,1024]{1,0:T(8,128)(2,1)S(1)} collective-permute-done((bf16[64,1024]{1,0:T(8,128)(2,1)S(1)}, bf16[64,1024]{1,0:T(8,128)(2,1)S(1)}, u32[]{:S(2)}, u32[]{:S(2)}) %collective-permute-start.7) | collective-permute-done | bytes 131104 | tf_op jit(solution)/shard_map/ppermute | solution.py:235
  52.6 1.9 %collective-permute-done.8 = bf16[64,1024]{1,0:T(8,128)(2,1)S(1)} collective-permute-done((bf16[64,1024]{1,0:T(8,128)(2,1)S(1)}, bf16[64,1024]{1,0:T(8,128)(2,1)S(1)}, u32[]{:S(2)}, u32[]{:S(2)}) %collective-permute-start.8) | collective-permute-done | bytes 131104 | tf_op jit(solution)/shard_map/ppermute | solution.py:239
  54.6 0.1 add_convert_fusion
  54.6 0.1 reshape.13
  54.7 12.7 %all_to_all.10 = bf16[16,4,1024]{2,1,0:T(4,128)(2,1)S(1)} all-to-all(bf16[16,4,1024]{2,1,0:T(4,128)(2,1)S(1)} %reshape.13), channel_id=1, replica_groups=mesh['row'=16,'tp'=16] {'row'}, dimensions={0} | all-to-all | bytes 262144 | tf_op jit(solution)/shard_map/all_to_all | solution.py:241
  67.4 0.7 %reshape.15 = bf16[1,8,8,1024]{3,2,1,0:T(8,128)(2,1)} reshape(bf16[8,2,4,1024]{3,2,1,0:T(4,128)(2,1)S(1)} %bitcast.33) | data formatting | bytes 262144 | tf_op jit(solution)/shard_map/reshape | solution.py:242
  (6 shorter events, 0.2 us)
Async XLA Ops:
  0.0 27.8 %copy-start = (bf16[3,256,1024]{2,1,0:T(8,128)(2,1)S(1)}, bf16[3,256,1024]{2,1,0:T(8,128)(2,1)}, u32[]{:S(2)}) copy-start(bf16[3,256,1024]{2,1,0:T(8,128)(2,1)} %unite_ref.3) | copy-start | bytes 4718596
  0.0 1.2 %copy-start.2 = (bf16[1,8,128,256]{3,2,1,0:T(8,128)(2,1)S(1)}, bf16[1,8,128,256]{3,2,1,0:T(8,128)(2,1)}, u32[]{:S(2)}) copy-start(bf16[1,8,128,256]{3,2,1,0:T(8,128)(2,1)} %param.4) | copy-start | bytes 1572868
  1.2 26.6 %copy-start.3 = (f32[3,256]{1,0:T(4,128)S(1)}, f32[3,256]{1,0:T(4,128)}, u32[]{:S(2)}) copy-start(f32[3,256]{1,0:T(4,128)} %bias_ref.7) | copy-start | bytes 9220
  2.1 25.3 %all-to-all-start = ((bf16[16,64,256]{2,1,0:T(8,128)(2,1)}), bf16[16,64,256]{2,1,0:T(8,128)(2,1)S(1)}, u32[]{:S(2)}, u32[]{:S(2)}) async-start(bf16[16,64,256]{2,1,0:T(8,128)(2,1)} %pack.1), calls=%async_computation | async-start | bytes 1048576 | tf_op jit(solution)/shard_map/all_to_all | solution.py:216
  11.8 1.2 %copy-start.1 = (bf16[3,4,64,576]{3,2,1,0:T(8,128)(2,1)S(1)}, bf16[3,4,64,576]{3,2,1,0:T(8,128)(2,1)}, u32[]{:S(2)}) copy-start(bf16[3,4,64,576]{3,2,1,0:T(8,128)(2,1)} %param.5) | copy-start | bytes 2654212
  30.2 3.1 %collective-permute-start.3 = (bf16[2,64,1024]{2,1,0:T(8,128)(2,1)S(1)}, bf16[2,64,1024]{2,1,0:T(8,128)(2,1)S(1)}, u32[]{:S(2)}, u32[]{:S(2)}) collective-permute-start(bf16[2,64,1024]{2,1,0:T(8,128)(2,1)S(1)} %get-tuple-element.27), channel_id=1, source_target_pairs={{0,1},{1,0},{2,3},{3,2},{4,5},{5,4},{6,7},{7,6},{8,9},{9,8},{10,11... | collective-permute-start | bytes 786440 | tf_op jit(solution)/shard_map/ppermute | solution.py:225
  32.8 6.2 %collective-permute-start = (bf16[2,64,1024]{2,1,0:T(8,128)(2,1)S(1)}, bf16[2,64,1024]{2,1,0:T(8,128)(2,1)S(1)}, u32[]{:S(2)}, u32[]{:S(2)}) collective-permute-start(bf16[2,64,1024]{2,1,0:T(8,128)(2,1)S(1)} %get-tuple-element.22), channel_id=1, source_target_pairs={{0,1},{1,0},{2,3},{3,2},{4,5},{5,4},{6,7},{7,6},{8,9},{9,8},{10,11... | collective-permute-start | bytes 786440 | tf_op jit(solution)/shard_map/ppermute | solution.py:225
  33.4 9.8 %collective-permute-start.5 = (bf16[2,64,1024]{2,1,0:T(8,128)(2,1)S(1)}, bf16[2,64,1024]{2,1,0:T(8,128)(2,1)S(1)}, u32[]{:S(2)}, u32[]{:S(2)}) collective-permute-start(bf16[2,64,1024]{2,1,0:T(8,128)(2,1)S(1)} %far.3.refs_0_), channel_id=1, source_target_pairs={{0,2},{1,3},{2,0},{3,1},{4,6},{5,7},{6,4},{7,5},{8,10},{9,11},{10,... | collective-permute-start | bytes 786440 | tf_op jit(solution)/shard_map/ppermute | solution.py:229
  38.8 4.4 %collective-permute-start.4 = (bf16[2,64,1024]{2,1,0:T(8,128)(2,1)S(1)}, bf16[2,64,1024]{2,1,0:T(8,128)(2,1)S(1)}, u32[]{:S(2)}, u32[]{:S(2)}) collective-permute-start(bf16[2,64,1024]{2,1,0:T(8,128)(2,1)S(1)} %get-tuple-element.29), channel_id=1, source_target_pairs={{0,1},{1,0},{2,3},{3,2},{4,5},{5,4},{6,7},{7,6},{8,9},{9,8},{10,11... | collective-permute-start | bytes 786440 | tf_op jit(solution)/shard_map/ppermute | solution.py:225
  39.0 10.3 %collective-permute-start.1 = (bf16[2,64,1024]{2,1,0:T(8,128)(2,1)S(1)}, bf16[2,64,1024]{2,1,0:T(8,128)(2,1)S(1)}, u32[]{:S(2)}, u32[]{:S(2)}) collective-permute-start(bf16[2,64,1024]{2,1,0:T(8,128)(2,1)S(1)} %far.2.refs_0_), channel_id=1, source_target_pairs={{0,2},{1,3},{2,0},{3,1},{4,6},{5,7},{6,4},{7,5},{8,10},{9,11},{10,... | collective-permute-start | bytes 786440 | tf_op jit(solution)/shard_map/ppermute | solution.py:232
  42.1 7.2 %collective-permute-start.2 = (bf16[2,64,1024]{2,1,0:T(8,128)(2,1)S(1)}, bf16[2,64,1024]{2,1,0:T(8,128)(2,1)S(1)}, u32[]{:S(2)}, u32[]{:S(2)}) collective-permute-start(bf16[2,64,1024]{2,1,0:T(8,128)(2,1)S(1)} %get-tuple-element.24), channel_id=1, source_target_pairs={{0,1},{1,0},{2,3},{3,2},{4,5},{5,4},{6,7},{7,6},{8,9},{9,8},{10,11... | collective-permute-start | bytes 786440 | tf_op jit(solution)/shard_map/ppermute | solution.py:225
  43.3 7.9 %collective-permute-start.6 = (bf16[64,1024]{1,0:T(8,128)(2,1)S(1)}, bf16[64,1024]{1,0:T(8,128)(2,1)S(1)}, u32[]{:S(2)}, u32[]{:S(2)}) collective-permute-start(bf16[64,1024]{1,0:T(8,128)(2,1)S(1)} %get-tuple-element.30), channel_id=1, source_target_pairs={{0,8},{1,9},{2,10},{3,11},{4,12},{5,13},{6,14},{7,15},{8,0},{9,1},... | collective-permute-start | bytes 393224 | tf_op jit(solution)/shard_map/ppermute | solution.py:235
  44.8 7.8 %collective-permute-start.7 = (bf16[64,1024]{1,0:T(8,128)(2,1)S(1)}, bf16[64,1024]{1,0:T(8,128)(2,1)S(1)}, u32[]{:S(2)}, u32[]{:S(2)}) collective-permute-start(bf16[64,1024]{1,0:T(8,128)(2,1)S(1)} %get-tuple-element.31), channel_id=1, source_target_pairs={{0,12},{1,13},{2,14},{3,15},{4,0},{5,1},{6,2},{7,3},{8,4},{9,5},{1... | collective-permute-start | bytes 393224 | tf_op jit(solution)/shard_map/ppermute | solution.py:235
  49.4 5.2 %collective-permute-start.8 = (bf16[64,1024]{1,0:T(8,128)(2,1)S(1)}, bf16[64,1024]{1,0:T(8,128)(2,1)S(1)}, u32[]{:S(2)}, u32[]{:S(2)}) collective-permute-start(bf16[64,1024]{1,0:T(8,128)(2,1)S(1)} %get-tuple-element.32), channel_id=1, source_target_pairs={{0,4},{1,5},{2,6},{3,7},{4,8},{5,9},{6,10},{7,11},{8,12},{9,13},{1... | collective-permute-start | bytes 393224 | tf_op jit(solution)/shard_map/ppermute | solution.py:239
